TPU v7x, 128 devices: a whole 4x4x4 slice. The times are simulated.
128 devices in a mesh: head: 8 (over y_lo, x), blk: 16 (over y_hi, z, core).
Axes of the slice: x: 4, y: 4 (y_hi: 2, y_lo: 2; y = y_hi * 2 + y_lo), z: 4, core: 2. Of those that a mesh axis runs over, the one named last changes fastest.
Arguments:
- queries: bfloat16 [32768, 1024], P(('blk', 'head'))
- key_in: bfloat16 [32768, 1024], P(('blk', 'head'))
- values: bfloat16 [32768, 1024], P(('blk', 'head')), may hold values from -6 to 6
- grad_out: bfloat16 [32768, 1024], P(('blk', 'head')), may hold values from -6 to 6
- block_list: int32 [256, 16], replicated, may hold values from 0 to 255, as said below
Outputs:
- grad_query: bfloat16 [32768, 1024], P(('blk', 'head'))
- grad_key: bfloat16 [32768, 1024], P(('blk', 'head'))
- grad_value: bfloat16 [32768, 1024], P(('blk', 'head'))
Inputs may be any that keep to these rules, and one draw needn't show every extreme that they name: `block_list`: the first four entries of row b are b, b - 1, b - 2, b - 3, each raised to 0 where negative; every other entry is a multiple of 16 not above b; entries may repeat.
All inputs are finite; a program needn't handle non-finite values.
Results may differ from a plain program's by a relative error of at most 0.024.
Values may be sent and summed in bfloat16 or wider, within the bound.
A program may use at most 192 MiB of HBM per device.

v0:
```python
import math

import jax
import jax.numpy as jnp
from jax import lax
from jax.sharding import PartitionSpec as P

DH = 128
QBLK = 128
MAXB = 16


def body(queries, key_in, values, grad_out, block_list):
    local_q, local_k, local_v, local_g = (
        lax.all_to_all(queries, "head", split_axis=1, concat_axis=0, tiled=True),
        lax.all_to_all(key_in, "head", split_axis=1, concat_axis=0, tiled=True),
        lax.all_to_all(values, "head", split_axis=1, concat_axis=0, tiled=True),
        lax.all_to_all(grad_out, "head", split_axis=1, concat_axis=0, tiled=True),
    )
    row_total = local_q.shape[0]
    row_width = local_q.shape[1]
    head_local = row_width // DH
    seg_blocks = row_total // QBLK
    own_index = lax.axis_index("blk")
    first_block = own_index * seg_blocks
    score_scale = 1.0 / math.sqrt(DH)
    block_rows = lax.dynamic_slice_in_dim(block_list, first_block, seg_blocks, 0)
    repeated = block_rows[:, :, None] == block_rows[:, None, :]
    first_seen = jnp.logical_not(jnp.any(jnp.tril(repeated, -1), axis=2))
    offsets = jnp.arange(QBLK, dtype=jnp.int32)
    query_pos = (first_block + jnp.arange(seg_blocks, dtype=jnp.int32))[:, None] * QBLK + offsets[
        None, :
    ]
    key_pos = block_rows[:, :, None] * QBLK + offsets[None, None, :]
    live_mask = first_seen[:, None, :, None] & (
        key_pos[:, None, :, :] <= query_pos[:, :, None, None]
    )
    live_mask = live_mask[:, None]
    own_pair = jnp.stack((local_k, local_v)).reshape(2, seg_blocks, QBLK, row_width)
    kv_table = lax.all_gather(own_pair, "blk", axis=1, tiled=True)
    flat_slots = block_rows.reshape(-1)
    chosen = kv_table[:, flat_slots].reshape(2, seg_blocks, MAXB, QBLK, head_local, DH)
    keys_sel = chosen[0]
    values_sel = chosen[1]
    query_blocks = local_q.reshape(seg_blocks, QBLK, head_local, DH)
    grad_blocks = local_g.reshape(seg_blocks, QBLK, head_local, DH)
    scores = (
        jnp.einsum("sqhd,smkhd->shqmk", query_blocks, keys_sel, preferred_element_type=jnp.float32)
        * score_scale
    )
    highest = jnp.max(jnp.where(live_mask, scores, -1e30), axis=(3, 4))
    weights = jnp.where(live_mask, jnp.exp(scores - highest[..., None, None]), 0.0)
    totals = jnp.sum(weights, axis=(3, 4))
    log_total = highest + jnp.log(totals)
    output = jnp.einsum(
        "shqmk,smkhd->sqhd", weights / totals[..., None, None], values_sel.astype(jnp.float32)
    ).astype(jnp.bfloat16)
    row_dot = jnp.transpose(
        jnp.sum(grad_blocks.astype(jnp.float32) * output.astype(jnp.float32), axis=-1), (0, 2, 1)
    )
    prob_tile = jnp.where(live_mask, jnp.exp(scores - log_total[..., None, None]), 0.0)
    probs_low = prob_tile.astype(jnp.bfloat16)
    value_part = jnp.einsum(
        "shqmk,sqhd->smkhd", probs_low, grad_blocks, preferred_element_type=jnp.float32
    )
    grad_prob = jnp.einsum(
        "sqhd,smkhd->shqmk", grad_blocks, values_sel, preferred_element_type=jnp.float32
    )
    grad_score = (prob_tile * (grad_prob - row_dot[..., None, None])).astype(jnp.bfloat16)
    query_grad = (
        jnp.einsum("shqmk,smkhd->sqhd", grad_score, keys_sel, preferred_element_type=jnp.float32)
        * score_scale
    ).astype(jnp.bfloat16)
    key_part = (
        jnp.einsum(
            "shqmk,sqhd->smkhd", grad_score, query_blocks, preferred_element_type=jnp.float32
        )
        * score_scale
    )
    grad_parts = jnp.stack((key_part, value_part)).reshape(2, seg_blocks * MAXB, QBLK, row_width)
    buffer = (
        jnp.zeros((2, kv_table.shape[1], QBLK, row_width), jnp.float32)
        .at[:, flat_slots]
        .add(grad_parts)
    )
    own_grad = lax.psum_scatter(buffer, "blk", scatter_dimension=1, tiled=True)
    grad_pairs = own_grad.reshape(2, row_total, row_width).astype(jnp.bfloat16)
    return (
        lax.all_to_all(
            query_grad.reshape(row_total, row_width),
            "head",
            split_axis=0,
            concat_axis=1,
            tiled=True,
        ),
        lax.all_to_all(grad_pairs[0], "head", split_axis=0, concat_axis=1, tiled=True),
        lax.all_to_all(grad_pairs[1], "head", split_axis=0, concat_axis=1, tiled=True),
    )


def solution(mesh):
    placed = (
        P(("blk", "head"), None),
        P(("blk", "head"), None),
        P(("blk", "head"), None),
        P(("blk", "head"), None),
        P(),
    )
    return jax.shard_map(
        body,
        mesh=mesh,
        in_specs=placed,
        out_specs=(P(("blk", "head"), None), P(("blk", "head"), None), P(("blk", "head"), None)),
        check_vma=False,
    )
```

profile of v0, /device:TPU:97, one launch (start us, length us, event | category | flops | bytes accessed | tf_op | source)
XLA Modules:
  0.0 652.2 jit_solution(1754850822968185614)
XLA Ops:
  7.2 0.0 copy-start
  7.2 2.1 copy.75
  9.3 5.0 all-to-all-start
  14.3 2.0 copy.77
  16.4 8.2 %all-to-all-done = bf16[256,8,128]{0,2,1:T(8,128)(2,1)S(1)} async-done(((bf16[256,8,128]{0,2,1:T(8,128)(2,1)}), bf16[256,8,128]{0,2,1:T(8,128)(2,1)S(1)}, u32[]{:S(2)}, u32[]{:S(2)}) %all-to-all-start) | async-done | bytes 524320 | tf_op jit(solution)/shard_map/all_to_all | solution.py:16
  24.5 3.5 all-to-all-start.1
  28.0 0.0 all-gather.2.cloned.1.call-start
  28.1 0.3 copy.76
  28.3 9.8 %all-to-all-done.1 = bf16[256,8,128]{0,2,1:T(8,128)(2,1)S(1)} async-done(((bf16[256,8,128]{0,2,1:T(8,128)(2,1)}), bf16[256,8,128]{0,2,1:T(8,128)(2,1)S(1)}, u32[]{:S(2)}, u32[]{:S(2)}) %all-to-all-start.1) | async-done | bytes 524320 | tf_op jit(solution)/shard_map/all_to_all | solution.py:17
  38.2 0.3 copy.78
  38.4 1.1 pad_maximum_fusion
  39.5 0.0 all-gather.2.cloned.1.call-update
  39.5 2.0 copy.84
  41.6 3.5 all-to-all-start.3
  45.1 0.8 broadcast_multiply_fusion
  45.9 0.1 copy.82
  45.9 0.1 copy.79
  46.0 0.1 reshape.227
  46.1 0.1 iota_compare_fusion
  46.2 0.4 select_reduce_fusion
  46.7 0.1 iota_add_fusion
  46.8 0.1 iota_add_fusion.1
  46.8 0.9 copy_bitcast_fusion.2
  47.7 7.6 %all-to-all-done.3 = bf16[256,8,128]{0,2,1:T(8,128)(2,1)S(1)} async-done(((bf16[256,8,128]{0,2,1:T(8,128)(2,1)}), bf16[256,8,128]{0,2,1:T(8,128)(2,1)S(1)}, u32[]{:S(2)}, u32[]{:S(2)}) %all-to-all-start.3) | async-done | bytes 524320 | tf_op jit(solution)/shard_map/all_to_all | solution.py:18
  55.3 3.5 all-to-all-start.2
  58.8 0.2 reduce-scatter.5.cloned.1.call-start
  59.1 1.0 copy.85
  60.1 0.1 bitcast_convert_fusion
  60.2 0.3 copy.86
  60.5 0.3 copy.89
  60.8 92.9 %all-gather.2.cloned.1.call-done = bf16[2,256,128,128]{3,2,1,0:T(8,128)(2,1)} async-done(((bf16[2,16,128,128]{3,2,1,0:T(8,128)(2,1)}), bf16[2,256,128,128]{3,2,1,0:T(8,128)(2,1)}) %all-gather.2.cloned.1.call-update) | async-done | bytes 16777232 | tf_op jit(solution)/shard_map/all_gather | solution.py:40
  153.7 15.5 %gather_fusion = bf16[256,2,128,128]{3,2,1,0:T(8,128)(2,1)} fusion(bf16[2,256,128,128]{3,2,1,0:T(8,128)(2,1)} %all-gather.2.cloned.1.call-done, s32[1024]{0:T(1024)S(1)} %pad_clamp_fusion), kind=kCustom, calls=%fused_computation | custom fusion | bytes 33555456 | tf_op jit(solution)/shard_map/gather | solution.py:42
  169.2 11.9 %fusion.53 = (bf16[1,256,128,128]{3,2,0,1:T(8,128)(2,1)}, bf16[1,256,128,128]{3,2,0,1:T(8,128)(2,1)}) fusion(bf16[2,256,128,128]{3,2,0,1:T(8,128)(2,1)} %bitcast.176), kind=kLoop, calls=%fused_computation.64 | loop fusion | bytes 33554432 | tf_op jit(solution)/shard_map/slice | solution.py:44
  181.1 0.0 all-to-all-done.2
  181.1 11.3 %fusion.1 = (f32[16,128]{1,0:T(8,128)S(1)}, f32[16,16,128,128]{3,2,1,0:T(8,128)S(1)}) fusion(s32[16,128]{1,0:T(8,128)S(1)} %iota_add_fusion.1, s32[16,16,128]{2,1,0:T(8,128)S(1)} %iota_add_fusion, pred[16,16]{1,0:T(8,128)(4,1)S(1)} %not.7, bf16[16,16,128,128]{3,2,1,0:T(8,128)(2,1)} %bitcast.177, bf16[16,128,128,1]{2,1,3,0:T(8,128)(2,1)S(1)} %bitcast.186), kind=kOutput, calls=%fused_computation.9 | convolution fusion | flops 1094711296 | bytes 25837824 | tf_op jit(solution)/shard_map/sqhd,smkhd->shqmk/dot_general | solution.py:48
  192.4 0.0 slice-start
  192.4 0.0 slice-start.1
  192.4 6.5 fusion.10
  199.0 0.0 copy-start.2
  199.0 11.1 %fusion.46 = f32[16,128]{1,0:T(8,128)S(1)} fusion(f32[16,128,1,128]{1,3,0,2:T(8,128)S(1)} %copy.89, bf16[16,16,128,128]{3,2,1,0:T(8,128)(2,1)S(1)} %bitcast.181, f32[16,16,128,128]{3,2,1,0:T(8,128)S(1)} %get-tuple-element.19, f32[16,128]{1,0:T(8,128)S(1)} %fusion.10, f32[16,128]{1,0:T(8,128)S(1)} %get-tuple-element.18, s32[16,128]{1,0:T(8,128)S(1)} %iota_add_fusion.1, ...), kind=kOutput, calls=%fused_computation.44 | convolution fusion | flops 1099954176 | bytes 26378496 | tf_op jit(solution)/shard_map/shqmk,smkhd->sqhd/dot_general | solution.py:55
  210.0 8.9 %fusion.11 = f32[16,16,128,128]{3,2,1,0:T(8,128)} fusion(bf16[16,128,128,1]{2,1,3,0:T(8,128)(2,1)S(1)} %bitcast.188, f32[16,16,128,128]{3,2,1,0:T(8,128)S(1)} %get-tuple-element.19, f32[16,128]{1,0:T(8,128)S(1)} %log_add_fusion, s32[16,128]{1,0:T(8,128)S(1)} %iota_add_fusion.1, s32[16,16,128]{2,1,0:T(8,128)S(1)} %iota_add_fusion, pred[16,16]{1,0:T(8,128)(4,1)S(1)} %not.7), kind=kOutput, calls=%fused_computation.20 | convolution fusion | flops 1098907648 | bytes 34226432 | tf_op jit(solution)/shard_map/shqmk,sqhd->smkhd/dot_general | solution.py:63
  219.0 9.7 %fusion = bf16[16,128,16,128]{1,3,2,0:T(8,128)(2,1)} fusion(f32[16,16,128,128]{3,2,1,0:T(8,128)S(1)} %get-tuple-element.19, bf16[16,16,128,128]{3,2,1,0:T(8,128)(2,1)S(1)} %bitcast.182, bf16[16,128,128,1]{2,1,3,0:T(8,128)(2,1)S(1)} %bitcast.189, f32[16,128]{1,0:T(8,128)S(1)} %fusion.46, f32[16,128]{1,0:T(8,128)S(1)} %log_add_fusion, ...), kind=kOutput, calls=%fused_computation.5 | convolution fusion | flops 1107296256 | bytes 34234624 | tf_op jit(solution)/shard_map/sqhd,smkhd->shqmk/dot_general | solution.py:66
  228.6 4.7 convolution_multiply_fusion
  233.4 18.4 %maximum_bitcast_fusion = f32[256,2,128,128]{3,2,1,0:T(8,128)} fusion(f32[1,256,128,128]{3,2,0,1:T(8,128)} %bitcast.175, f32[1,256,128,128]{3,2,0,1:T(8,128)S(1)} %bitcast.174), kind=kLoop, calls=%fused_computation.3 | loop fusion | flops 8388608 | bytes 67108864 | tf_op jit(solution)/shard_map/stack | solution.py:80
  251.8 11.2 %broadcast_in_dim.38 = f32[2,256,128,128]{3,2,1,0:T(8,128)} broadcast(f32[]{:T(128)} %constant.5.clone.1), dimensions={} | broadcast | bytes 33554436 | tf_op jit(solution)/shard_map/broadcast_in_dim | solution.py:82
  263.0 73.0 %scatter_fusion = f32[2,256,128,128]{3,2,1,0:T(8,128)} fusion(f32[2,256,128,128]{3,2,1,0:T(8,128)} %broadcast_in_dim.38, s32[256]{0:T(256)S(1)} %bitcast.201, f32[256,2,128,128]{3,2,1,0:T(8,128)} %maximum_bitcast_fusion), kind=kCustom, calls=%fused_computation.1 | custom fusion | flops 8388608 | bytes 100664320 | tf_op jit(solution)/shard_map/scatter-add | solution.py:84
  336.0 12.0 %copy.105 = f32[2,256,128,128]{3,2,0,1:T(8,128)S(1)} copy(f32[2,256,128,128]{3,2,1,0:T(8,128)} %scatter_fusion) | data formatting | bytes 67108864
  348.1 21.5 %copy.118 = f32[32,8,256,128]{3,1,2,0:T(8,128)} copy(f32[32,8,256,128]{3,2,1,0:T(8,128)S(1)} %bitcast.173) | data formatting | bytes 67108864
  369.6 0.0 reduce-scatter.5.cloned.1.call-update
  369.7 0.0 copy-start.1
  369.7 9.2 %fusion.30 = bf16[16,128,128]{1,2,0:T(8,128)(2,1)} fusion(bf16[16,16,128,128]{3,2,1,0:T(8,128)(2,1)} %bitcast.178, bf16[16,128,16,128]{1,3,2,0:T(8,128)(2,1)} %fusion), kind=kOutput, calls=%fused_computation.38 | convolution fusion | flops 1074266112 | bytes 17301504 | tf_op jit(solution)/shard_map/shqmk,smkhd->sqhd/dot_general | solution.py:71
  378.9 4.0 all-to-all-start.4
  382.9 234.6 %reduce-scatter.5.cloned.1.call-done = f32[16,32768]{1,0:T(8,128)} async-done(((f32[256,32768]{1,0:T(8,128)}), f32[16,32768]{1,0:T(8,128)}) %reduce-scatter.5.cloned.1.call-update) | async-done | bytes 2097168
  617.4 2.0 copy.110
  619.4 0.9 fusion.54
  620.3 0.0 all-to-all-done.4
  620.3 12.7 %all_to_all.121 = bf16[8,256,128]{2,1,0:T(8,128)(2,1)S(1)} all-to-all(bf16[8,256,128]{2,1,0:T(8,128)(2,1)S(1)} %bitcast.198), channel_id=1, replica_groups=mesh['head'=8,'blk'=16] {'head'}, dimensions={0} | all-to-all | bytes 1048576 | tf_op jit(solution)/shard_map/all_to_all | solution.py:96
  633.1 3.5 all-to-all-start.6
  636.6 0.9 copy_bitcast_fusion.1
  637.4 0.2 copy.94
  637.7 1.0 copy.96
  638.7 5.5 all-to-all-done.6
  644.1 0.2 copy.95
  644.4 1.0 copy.97
  (12 shorter events, 0.0 us)
Async XLA Ops:
  7.2 39.7 %copy-start = (bf16[256,1024]{1,0:T(8,128)(2,1)S(1)}, bf16[256,1024]{1,0:T(8,128)(2,1)}, u32[]{:S(2)}) copy-start(bf16[256,1024]{1,0:T(8,128)(2,1)} %param.5) | copy-start | bytes 1572868
  9.3 15.2 %all-to-all-start = ((bf16[256,8,128]{0,2,1:T(8,128)(2,1)}), bf16[256,8,128]{0,2,1:T(8,128)(2,1)S(1)}, u32[]{:S(2)}, u32[]{:S(2)}) async-start(bf16[256,8,128]{0,2,1:T(8,128)(2,1)} %bitcast), calls=%async_computation | async-start | bytes 1048576 | tf_op jit(solution)/shard_map/all_to_all | solution.py:16
  24.5 13.7 %all-to-all-start.1 = ((bf16[256,8,128]{0,2,1:T(8,128)(2,1)}), bf16[256,8,128]{0,2,1:T(8,128)(2,1)S(1)}, u32[]{:S(2)}, u32[]{:S(2)}) async-start(bf16[256,8,128]{0,2,1:T(8,128)(2,1)} %bitcast.3), calls=%async_computation.1 | async-start | bytes 1048576 | tf_op jit(solution)/shard_map/all_to_all | solution.py:17
  28.0 125.7 %all-gather.2.cloned.1.call-start = ((), (), s32[]{:S(2)}) async-start(), calls=%async_computation.8 | async-start | bytes 17825792 | tf_op jit(solution)/shard_map/all_gather | solution.py:40
  41.6 13.8 %all-to-all-start.3 = ((bf16[256,8,128]{0,2,1:T(8,128)(2,1)}), bf16[256,8,128]{0,2,1:T(8,128)(2,1)S(1)}, u32[]{:S(2)}, u32[]{:S(2)}) async-start(bf16[256,8,128]{0,2,1:T(8,128)(2,1)} %bitcast.15), calls=%async_computation.3 | async-start | bytes 1048576 | tf_op jit(solution)/shard_map/all_to_all | solution.py:18
  55.3 125.7 %all-to-all-start.2 = ((bf16[256,8,128]{2,0,1:T(8,128)(2,1)}), bf16[256,8,128]{2,0,1:T(8,128)(2,1)S(1)}, u32[]{:S(2)}, u32[]{:S(2)}) async-start(bf16[256,8,128]{2,0,1:T(8,128)(2,1)} %copy_bitcast_fusion.2), calls=%async_computation.2 | async-start | bytes 1048576 | tf_op jit(solution)/shard_map/all_to_all | solution.py:15
  58.8 558.6 %reduce-scatter.5.cloned.1.call-start = ((), (), s32[]{:S(2)}) async-start(), calls=%async_computation.9 | async-start | bytes 35651584
  192.4 6.6 %slice-start = ((s8[8388608]{0:T(1024)(128)(4,1)}), s8[4194304]{0:T(1024)(128)(4,1)S(1)}, s32[]{:S(2)}) async-start(s8[8388608]{0:T(1024)(128)(4,1)} %bitcast.179), calls=%async_computation.10 | async-start | bytes 8388608
  192.4 6.6 %slice-start.1 = ((s8[8388608]{0:T(1024)(128)(4,1)}), s8[4194304]{0:T(1024)(128)(4,1)S(1)}, s32[]{:S(2)}) async-start(s8[8388608]{0:T(1024)(128)(4,1)} %bitcast.179), calls=%async_computation.11 | async-start | bytes 8388608
  199.0 11.1 %copy-start.2 = (bf16[8,256,128]{2,1,0:T(8,128)(2,1)S(1)}, bf16[8,256,128]{2,1,0:T(8,128)(2,1)}, u32[]{:S(2)}) copy-start(bf16[8,256,128]{2,1,0:T(8,128)(2,1)} %copy.85) | copy-start | bytes 1572868
  369.7 275.7 %copy-start.1 = (bf16[256,1024]{1,0:T(8,128)(2,1)S(1)}, bf16[256,1024]{1,0:T(8,128)(2,1)}, u32[]{:S(2)}) copy-start(bf16[256,1024]{1,0:T(8,128)(2,1)} %param.5) | copy-start | bytes 1572868
  378.9 241.5 %all-to-all-start.4 = ((bf16[8,256,128]{2,1,0:T(8,128)(2,1)}), bf16[8,256,128]{2,1,0:T(8,128)(2,1)S(1)}, u32[]{:S(2)}, u32[]{:S(2)}) async-start(bf16[8,256,128]{2,1,0:T(8,128)(2,1)} %bitcast.30), calls=%async_computation.4 | async-start | bytes 1048576 | tf_op jit(solution)/shard_map/all_to_all | solution.py:89
  633.1 11.1 %all-to-all-start.6 = ((bf16[8,256,128]{2,1,0:T(8,128)(2,1)}), bf16[8,256,128]{2,1,0:T(8,128)(2,1)S(1)}, u32[]{:S(2)}, u32[]{:S(2)}) async-start(bf16[8,256,128]{2,1,0:T(8,128)(2,1)} %bitcast.51), calls=%async_computation.6 | async-start | bytes 1048576 | tf_op jit(solution)/shard_map/all_to_all | solution.py:97
Sparse Core Ops, SparseCore 0:
  39.6 114.0 all-gather.1
  369.8 247.6 reduce-scatter.4
where the time goes:
time: 660 us; the launch traced here: 652 us
  waiting for transfers between devices  359 us (54%)
  other arithmetic  101 us (15%)
  local copies, waits for them, and re-layouts  87.9 us (13%)
  matrix products  54.9 us (8%)
  starting transfers between devices  23.3 us (4%)
  between operations  14.3 us (2%)
  blocking collectives  12.7 us (2%)
    unnamed x3, waiting for transfers between devices  235 us
    all_gather x1, waiting for transfers between devices, body(): kv_table = lax.all_gather(own_pair, 'blk', axis=1, tiled=True)  92.9 us
    scatter-add x1, other arithmetic, body(): buffer = jnp.zeros((2, kv_table.shape[1], QBLK, row_width), jnp.float32)....  73 us
    unnamed x18, local copies, waits for them, and re-layouts  43.8 us
    another operation x1, other arithmetic, body(): jnp.stack((key_part, value_part))  18.4 us
    gather x1, local copies, waits for them, and re-layouts, body(): kv_table[:, flat_slots].reshape(2, seg_blocks, MAXB, QBLK, head_local, DH)  15.5 us
  transfers between devices with their start and end apart: 8, of which 6 were waited for; matrix products, arithmetic and copies ran while one was open for 8% of the time, Pallas kernels for 0%

commit v1 on v0

v1 whole, which is shorter than its diff:
```python
import math

import jax
import jax.numpy as jnp
from jax import lax
from jax.experimental import pallas as pl
from jax.experimental.pallas import tpu as pltpu
from jax.sharding import PartitionSpec as P

DH = 128
QBLK = 128
MAXB = 16
SEGB = 16
HALO = 3 * QBLK
CHUNK = 2 * QBLK
MESH = pl.DeviceIdType.MESH
VMEM = pltpu.VMEM
BF16 = jnp.bfloat16
F32 = jnp.float32
DEAD = -3e38
NT = (((1,), (1,)), ((), ()))


def rows_of(start, size):
    return pl.ds(pl.multiple_of(start, QBLK), size)


def remote(src, dst, send, recv, **where):
    return pltpu.make_async_remote_copy(
        src_ref=src,
        dst_ref=dst,
        send_sem=send,
        recv_sem=recv,
        device_id=where,
        device_id_type=MESH,
    )


def greet(heads, blks):
    head, blk = lax.axis_index("head"), lax.axis_index("blk")
    barrier = pltpu.get_barrier_semaphore()
    for step in range(1, heads):
        pl.semaphore_signal(
            barrier, inc=1, device_id={"head": lax.rem(head + step, heads)}, device_id_type=MESH
        )
    for step in range(1, blks):
        pl.semaphore_signal(
            barrier, inc=1, device_id={"blk": lax.rem(blk + step, blks)}, device_id_type=MESH
        )
    pl.semaphore_wait(barrier, heads + blks - 2)


def gather_kernel(
    heads, blks, q, k, v, g, lq, lk, lv, lg, sk, sv, send_in, recv_in, send_sum, recv_sum, send_halo, recv_halo
):
    head, blk = lax.axis_index("head"), lax.axis_index("blk")
    part = q.shape[0]
    rows = heads * part
    arrays = ((k, lk, HALO), (v, lv, HALO), (q, lq, 0), (g, lg, 0))
    greet(heads, blks)

    def into(which, source, there):
        src, dst, skip = arrays[which]
        return remote(
            src.at[:, rows_of(there * DH, DH)],
            dst.at[rows_of(skip + source * part, part)],
            send_in.at[which, there],
            recv_in.at[which, source],
            head=there,
        )

    for which in range(4):
        for step in range(1, heads):
            into(which, head, lax.rem(head + step, heads)).start()
    for src, dst, skip in arrays:
        dst[rows_of(skip + head * part, part), :] = src[:, rows_of(head * DH, DH)]

    def arrive(which, source):
        @pl.when(head != source)
        def _():
            into(which, source, head).wait_recv()

    pairs = ((lk, sk), (lv, sv))

    def summary(which, owner, there):
        src, dst = pairs[which]
        return remote(
            src.at[pl.ds(HALO, QBLK)],
            dst.at[rows_of(owner * QBLK, QBLK)],
            send_sum.at[which, there],
            recv_sum.at[which, owner],
            blk=there,
        )

    def halo(which, there):
        src, _ = pairs[which]
        return remote(
            src.at[pl.ds(rows, HALO)], src.at[pl.ds(0, HALO)], send_halo.at[which], recv_halo.at[which], blk=there
        )

    for which in range(2):
        arrive(which, 0)
        src, dst = pairs[which]
        for step in range(1, blks):
            @pl.when(blk + step < blks)
            def _():
                summary(which, blk, blk + step).start()

        for owner in range(blks):
            @pl.when(owner > blk)
            def _():
                dst[pl.ds(owner * QBLK, QBLK), :] = jnp.zeros((QBLK, DH), BF16)

        dst[rows_of(blk * QBLK, QBLK), :] = src[pl.ds(HALO, QBLK), :]

        for source in range(1, heads):
            arrive(which, source)

        @pl.when(blk + 1 < blks)
        def _():
            halo(which, blk + 1).start()

        @pl.when(blk == 0)
        def _():
            src[pl.ds(0, HALO), :] = jnp.zeros((HALO, DH), BF16)

    for which in range(2, 4):
        for source in range(heads):
            arrive(which, source)

    for which in range(2):
        for step in range(1, blks):
            @pl.when(blk + step < blks)
            def _():
                summary(which, blk, blk + step).wait_send()

        for owner in range(blks - 1):
            @pl.when(owner < blk)
            def _():
                summary(which, owner, blk).wait_recv()

        @pl.when(blk + 1 < blks)
        def _():
            halo(which, blk + 1).wait_send()

        @pl.when(blk > 0)
        def _():
            halo(which, blk).wait_recv()

    for which in range(4):
        for step in range(1, heads):
            into(which, head, lax.rem(head + step, heads)).wait_send()


def attend_kernel(lists, q, k, v, g, sk, sv, dq, dk, dv, dsk, dsv, kt, skt, live, scores, gprob):
    blk = lax.axis_index("blk")
    rows = q.shape[0]
    keys = sk.shape[0]
    chunks = rows // CHUNK
    wide = HALO + CHUNK
    factor = 1.0 / math.sqrt(DH)
    exp2_factor = factor * math.log2(math.e)
    slabs = [(s, CHUNK) for s in range(0, keys, CHUNK)]

    for start in range(0, k.shape[0], QBLK):
        kt[:, pl.ds(start, QBLK)] = k[pl.ds(start, QBLK), :].T
    for start in range(0, keys, QBLK):
        skt[:, pl.ds(start, QBLK)] = sk[pl.ds(start, QBLK), :].T
    for ref in (dk, dv, dsk, dsv):
        ref[...] = jnp.zeros(ref.shape, ref.dtype)

    mine = lists[pl.ds(pl.multiple_of(blk * SEGB, SEGB), SEGB), :]
    summary = lax.broadcasted_iota(jnp.int32, (SEGB, MAXB), 0) * SEGB
    owner = lax.broadcasted_iota(jnp.int32, (SEGB, QBLK), 0) * SEGB
    for block in range(SEGB):
        hit = jnp.where(mine[block : block + 1, :] == summary, 1.0, 0.0)
        seen = jnp.broadcast_to(jnp.max(hit, axis=1, keepdims=True), (SEGB, QBLK))
        far = owner < blk * SEGB + block - 3
        live[block // 2, :, pl.ds((block % 2) * QBLK, QBLK)] = jnp.where(far, seen, 0.0)

    def chunk_step(c, carry):
        base = pl.multiple_of(c * CHUNK, CHUNK)
        here = pl.ds(base, CHUNK)
        window = pl.ds(base, wide)
        queries, grads = q[here, :], g[here, :]
        top = jnp.full((1, CHUNK), DEAD, F32)
        for start, size in slabs:
            raw = lax.dot_general(sk[pl.ds(start, size), :], queries, NT, preferred_element_type=F32)
            for sub in range(0, size, QBLK):
                alive = live[c, pl.ds((start + sub) // QBLK, 1), :] > 0.5
                masked = jnp.where(alive, raw[sub : sub + QBLK] * exp2_factor, DEAD)
                scores[pl.ds(start + sub, QBLK), :] = masked
                top = jnp.maximum(top, jnp.max(masked, axis=0, keepdims=True))
        key_row = lax.broadcasted_iota(jnp.int32, (wide, CHUNK), 0)
        query_row = lax.broadcasted_iota(jnp.int32, (wide, CHUNK), 1)
        alive = (
            (key_row <= query_row + HALO)
            & ((key_row >= QBLK) | (query_row < QBLK))
            & ((blk > 0) | (key_row + base >= HALO))
        )
        raw = lax.dot_general(k[window, :], queries, NT, preferred_element_type=F32)
        masked = jnp.where(alive, raw * exp2_factor, DEAD)
        scores[pl.ds(keys, wide), :] = masked
        top = jnp.maximum(top, jnp.max(masked, axis=0, keepdims=True))

        total = jnp.zeros((1, CHUNK), F32)
        dotted = jnp.zeros((1, CHUNK), F32)
        for start, size in slabs + [(keys, wide)]:
            there = v[window, :] if start == keys else sv[pl.ds(start, size), :]
            gp = lax.dot_general(there, grads, NT, preferred_element_type=F32)
            weight = jnp.exp2(scores[pl.ds(start, size), :] - top)
            scores[pl.ds(start, size), :] = weight
            gprob[pl.ds(start, size), :] = gp
            total += jnp.sum(weight, axis=0, keepdims=True)
            dotted += jnp.sum(weight * gp, axis=0, keepdims=True)
        inverse = 1.0 / total
        row_dot = dotted * inverse

        dq_t = jnp.zeros((DH, CHUNK), F32)
        for start, size in slabs + [(keys, wide)]:
            prob = scores[pl.ds(start, size), :] * inverse
            ds = (prob * (gprob[pl.ds(start, size), :] - row_dot)).astype(BF16)
            value_part = jnp.dot(prob.astype(BF16), grads, preferred_element_type=F32)
            key_part = jnp.dot(ds, queries, preferred_element_type=F32)
            if start == keys:
                dv[window, :] += value_part
                dk[window, :] += key_part
                turned = kt[:, window]
            else:
                dsv[pl.ds(start, size), :] += value_part
                dsk[pl.ds(start, size), :] += key_part
                turned = skt[:, pl.ds(start, size)]
            dq_t += jnp.dot(turned, ds, preferred_element_type=F32)
        dq[here, :] = (dq_t.T * factor).astype(BF16)
        return carry

    lax.fori_loop(0, chunks, chunk_step, 0)


def scatter_kernel(
    heads, blks, dq, dk, dv, dsk, dsv, oq, ok, ov,
    bk, bv, gk, gv, hk, hv, total, send_out, recv_out, send_sum, recv_sum, send_halo, recv_halo,
):
    head, blk = lax.axis_index("head"), lax.axis_index("blk")
    part = oq.shape[0]
    rows = heads * part
    factor = 1.0 / math.sqrt(DH)
    sets = ((dk, dsk, bk, gk, hk, ok, factor), (dv, dsv, bv, gv, hv, ov, 1.0))
    for own, own_sum, out, sums, _, _, scale in sets:
        sums[0] = (own_sum[...] * scale).astype(BF16)
        out[pl.ds(0, HALO), :] = (own[pl.ds(0, HALO), :] * scale).astype(BF16)
    greet(heads, blks)

    def summary(which, owner, source):
        sums = sets[which][3]
        return remote(
            sums.at[0, rows_of(owner * QBLK, QBLK)],
            sums.at[1, rows_of(source * QBLK, QBLK)],
            send_sum.at[which, owner],
            recv_sum.at[which, source],
            blk=owner,
        )

    def halo(which, there):
        _, _, out, _, into, _, _ = sets[which]
        return remote(out.at[pl.ds(0, HALO)], into, send_halo.at[which], recv_halo.at[which], blk=there)

    outs = ((dq, oq, 0), (bk, ok, HALO), (bv, ov, HALO))

    def back(which, source, there):
        src, dst, skip = outs[which]
        return remote(
            src.at[rows_of(skip + there * part, part)],
            dst.at[:, rows_of(source * DH, DH)],
            send_out.at[which, there],
            recv_out.at[which, source],
            head=there,
        )

    def send(which, there):
        src, dst, skip = outs[which]

        @pl.when(head != there)
        def _():
            back(which, head, there).start()

        @pl.when(head == there)
        def _():
            dst[:, rows_of(there * DH, DH)] = src[pl.ds(skip + there * part, part), :]

    for which in range(2):
        for owner in range(blks - 1):
            @pl.when(owner < blk)
            def _():
                summary(which, owner, blk).start()

        @pl.when(blk > 0)
        def _():
            halo(which, blk - 1).start()

    for there in range(heads):
        send(0, there)
    late = [(heads * part - HALO) // part, heads - 1]
    for which in range(2):
        own, _, out, _, _, _, scale = sets[which]
        for there in range(1, late[0]):
            at = pl.ds(HALO + there * part, part)
            out[at, :] = (own[at, :] * scale).astype(BF16)
            send(1 + which, there)
    for which in range(2):
        own, _, out, _, into, _, scale = sets[which]

        @pl.when(blk + 1 < blks)
        def _():
            halo(which, blk).wait_recv()

        first = HALO + late[0] * part
        spare = (heads - late[0]) * part - HALO
        if spare > 0:
            at = pl.ds(first, spare)
            out[at, :] = (own[at, :] * scale).astype(BF16)
        at = pl.ds(rows, HALO)

        @pl.when(blk + 1 < blks)
        def _():
            out[at, :] = (own[at, :] * scale + into[...].astype(F32)).astype(BF16)

        @pl.when(blk + 1 == blks)
        def _():
            out[at, :] = (own[at, :] * scale).astype(BF16)

        for there in range(late[0], heads):
            send(1 + which, there)
    for which in range(2):
        own, own_sum, out, sums, _, _, scale = sets[which]
        total[...] = own[pl.ds(HALO, QBLK), :] + own_sum[rows_of(blk * QBLK, QBLK), :]
        total[...] *= scale
        for source in range(1, blks):
            @pl.when(source > blk)
            def _():
                summary(which, blk, source).wait_recv()
                total[...] += sums[1, pl.ds(source * QBLK, QBLK), :].astype(F32)

        out[pl.ds(HALO, QBLK), :] = total[...].astype(BF16)
        at = pl.ds(HALO + QBLK, part - QBLK)
        out[at, :] = (own[at, :] * scale).astype(BF16)
        send(1 + which, 0)

    for which in range(2):
        for owner in range(blks - 1):
            @pl.when(owner < blk)
            def _():
                summary(which, owner, blk).wait_send()

        @pl.when(blk > 0)
        def _():
            halo(which, blk - 1).wait_send()

    for which in range(3):
        for step in range(1, heads):
            other = lax.rem(head + step, heads)
            back(which, head, other).wait_send()
            back(which, other, head).wait_recv()


def body_of(heads, blks):
    def body(queries, key_in, values, grad_out, block_list):
        part, width = queries.shape
        rows, keys = heads * part, blks * QBLK
        dma = pltpu.SemaphoreType.DMA
        whole = pl.BlockSpec(memory_space=VMEM)

        def shape(*dims, dtype=BF16):
            return jax.ShapeDtypeStruct(dims, dtype)

        comm = dict(has_side_effects=True, vmem_limit_bytes=48 * 1024 * 1024)
        lq, lk, lv, lg, sk, sv = pl.pallas_call(
            lambda *refs: gather_kernel(heads, blks, *refs),
            out_shape=(
                shape(rows, DH),
                shape(HALO + rows, DH),
                shape(HALO + rows, DH),
                shape(rows, DH),
                shape(keys, DH),
                shape(keys, DH),
            ),
            in_specs=[whole] * 4,
            out_specs=[whole] * 6,
            scratch_shapes=[
                dma((4, heads)),
                dma((4, heads)),
                dma((2, blks)),
                dma((2, blks)),
                dma((2,)),
                dma((2,)),
            ],
            compiler_params=pltpu.CompilerParams(collective_id=0, **comm),
            name="gather",
        )(queries, key_in, values, grad_out)
        wide = HALO + CHUNK
        dq, dk, dv, dsk, dsv = pl.pallas_call(
            attend_kernel,
            out_shape=(
                shape(rows, DH),
                shape(HALO + rows, DH, dtype=F32),
                shape(HALO + rows, DH, dtype=F32),
                shape(keys, DH, dtype=F32),
                shape(keys, DH, dtype=F32),
            ),
            in_specs=[whole] * 7,
            out_specs=[whole] * 5,
            scratch_shapes=[
                VMEM((DH, HALO + rows), BF16),
                VMEM((DH, keys), BF16),
                VMEM((rows // CHUNK, SEGB, CHUNK), F32),
                VMEM((keys + wide, CHUNK), F32),
                VMEM((keys + wide, CHUNK), F32),
            ],
            compiler_params=pltpu.CompilerParams(vmem_limit_bytes=48 * 1024 * 1024),
            name="attend",
        )(block_list, lq, lk, lv, lg, sk, sv)
        return pl.pallas_call(
            lambda *refs: scatter_kernel(heads, blks, *refs),
            out_shape=(shape(part, width),) * 3,
            in_specs=[whole] * 5,
            out_specs=[whole] * 3,
            scratch_shapes=[
                VMEM((HALO + rows, DH), BF16),
                VMEM((HALO + rows, DH), BF16),
                VMEM((2, keys, DH), BF16),
                VMEM((2, keys, DH), BF16),
                VMEM((HALO, DH), BF16),
                VMEM((HALO, DH), BF16),
                VMEM((QBLK, DH), F32),
                dma((3, heads)),
                dma((3, heads)),
                dma((2, blks)),
                dma((2, blks)),
                dma((2,)),
                dma((2,)),
            ],
            compiler_params=pltpu.CompilerParams(collective_id=1, **comm),
            name="scatter",
        )(dq, dk, dv, dsk, dsv)

    return body


def solution(mesh):
    placed = P(("blk", "head"), None)
    return jax.shard_map(
        body_of(mesh.shape["head"], mesh.shape["blk"]),
        mesh=mesh,
        in_specs=(placed,) * 4 + (P(),),
        out_specs=(placed,) * 3,
        check_vma=False,
    )
```

time: 660 us -> 125 us (0.19); the launches traced: 652 us -> 124 us
  waiting for transfers between devices: 359 us -> 0 us
  Pallas kernels: 0 us -> 115 us
  other arithmetic: 101 us -> 0 us
  local copies, waits for them, and re-layouts: 87.9 us -> 8.65 us
  matrix products: 54.9 us -> 0 us
  starting transfers between devices: 23.3 us -> 0 us
  between operations: 14.3 us -> 0.66 us
  blocking collectives: 12.7 us -> 0 us
    unnamed x3 -> x0, waiting for transfers between devices: 235 us -> none
    pallas_call x0 -> x3, Pallas kernels: none -> 115 us  [the longest x1 47.5 us: body(): pl.pallas_call(lambda *refs: scatter_kernel(heads, blks, *refs), out_shap...]
    all_gather x1 -> x0, waiting for transfers between devices: 92.9 us -> none  [body(): kv_table = lax.all_gather(own_pair, 'blk', axis=1, tiled=True)]
    scatter-add x1 -> x0, other arithmetic: 73 us -> none  [body(): buffer = jnp.zeros((2, kv_table.shape[1], QBLK, row_width), jnp.float32)....]
    dot_general x6 -> x0, matrix products: 54.9 us -> none  [the longest x1 11.3 us: body(): jnp.einsum('sqhd,smkhd->shqmk', query_blocks, keys_sel, preferred_element...]
    unnamed x18 -> x14, local copies, waits for them, and re-layouts: 43.8 us -> 8.65 us
    all_to_all x6 -> x0, waiting for transfers between devices: 31.1 us -> none  [the longest x1 9.83 us: body(): lax.all_to_all(values, 'head', split_axis=1, concat_axis=0, tiled=True)]
    all_to_all x6 -> x0, starting transfers between devices: 23 us -> none  [the longest x1 5.03 us: body(): lax.all_to_all(key_in, 'head', split_axis=1, concat_axis=0, tiled=True)]
  transfers between devices with their start and end apart: 8 -> 0, of which waited for: 6 -> 0; matrix products, arithmetic and copies ran while one was open for 8% -> 0% of each run, Pallas kernels for 0% -> 0%
where the time goes in v1:
time: 125 us; the launch traced here: 124 us
  Pallas kernels  115 us (92%)
  local copies, waits for them, and re-layouts  8.65 us (7%)
    pallas_call x1, Pallas kernels, body(): pl.pallas_call(lambda *refs: scatter_kernel(heads, blks, *refs), out_shap...  47.5 us
    pallas_call x1, Pallas kernels, body(): pl.pallas_call(lambda *refs: gather_kernel(heads, blks, *refs), out_shape...  41.5 us
    pallas_call x1, Pallas kernels, body(): pl.pallas_call(attend_kernel, out_shape=(shape(rows, DH), shape(HALO + ro...  26.1 us
    unnamed x14, local copies, waits for them, and re-layouts  8.65 us

profile of v1, /device:TPU:97, one launch (start us, length us, event | category | flops | bytes accessed | tf_op | source)
XLA Modules:
  0.0 124.4 jit_solution(5853474218718707)
XLA Ops:
  0.6 0.8 copy.8.lists
  1.4 0.0 copy-start.1
  1.5 1.0 copy-done.1
  2.5 0.0 copy-start.2
  2.5 1.0 copy-done.2
  3.5 0.0 copy-start.3
  3.5 1.0 copy-done.3
  4.6 0.0 copy-start.4
  4.6 1.0 copy-done.4
  5.6 41.5 %gather.1 = (bf16[2048,128]{1,0:T(8,128)(2,1)S(1)}, bf16[2432,128]{1,0:T(8,128)(2,1)S(1)}, bf16[2432,128]{1,0:T(8,128)(2,1)S(1)}, bf16[2048,128]{1,0:T(8,128)(2,...) custom-call(bf16[256,1024]{1,0:T(8,128)(2,1)S(1)} %copy-done.1, bf16[256,1024]{1,0:T(8,128)(2,1)S(1)} %copy-done.2, ...), custom_call_target="tpu_custom_call" | custom-call | tf_op jit(solution)/shard_map/gather/pallas_call | solution.py:377
  47.1 26.1 %attend.1 = (bf16[2048,128]{1,0:T(8,128)(2,1)S(1)}, f32[2432,128]{1,0:T(8,128)}, f32[2432,128]{1,0:T(8,128)}, f32[2048,128]{1,0:T(8,128)S(1)}, f32[2048,128]{1,0:T(8,128)S(1)}) custom-call(s32[256,16]{1,0:T(8,128)S(1)} %copy.8.lists, bf16[2048,128]{1,0:T(8,128)(2,1)S(1)} %get-tuple-element.14.q, bf16[2432,128]{1,0:T(8,128)(2,1)S(1)} %get-tuple-element.15.k, ...), custom_call_target="tpu_custom_call" | custom-call | tf_op jit(solution)/shard_map/attend/pallas_call | solution.py:401
  73.2 0.0 copy-start
  73.2 1.3 %copy-done = f32[2432,128]{1,0:T(8,128)S(1)} copy-done((f32[2432,128]{1,0:T(8,128)S(1)}, f32[2432,128]{1,0:T(8,128)}, u32[]{:S(2)}) %copy-start) | copy-done | bytes 1245208
  74.5 47.5 %scatter.1 = (bf16[256,1024]{1,0:T(8,128)(2,1)S(1)}, bf16[256,1024]{1,0:T(8,128)(2,1)S(1)}, bf16[256,1024]{1,0:T(8,128)(2,1)S(1)}) custom-call(bf16[2048,128]{1,0:T(8,128)(2,1)S(1)} %get-tuple-element.20.refs_0_, f32[2432,128]{1,0:T(8,128)S(1)} %copy-done, f32[2432,128]{1,0:T(8,128)} %get-tuple-element.22.refs_2_, ...), custom_call_target="tpu_custom_call" | custom-call | tf_op jit(solution)/shard_map/scatter/pallas_call | solution.py:422
  122.0 0.8 copy.12
  122.8 0.8 copy.13
  123.6 0.8 copy.14
Async XLA Ops:
  1.4 1.0 copy-start.1
  2.5 1.0 copy-start.2
  3.5 1.0 copy-start.3
  4.6 1.0 copy-start.4
  73.2 1.3 %copy-start = (f32[2432,128]{1,0:T(8,128)S(1)}, f32[2432,128]{1,0:T(8,128)}, u32[]{:S(2)}) copy-start(f32[2432,128]{1,0:T(8,128)} %get-tuple-element.21.refs_1_) | copy-start | bytes 3735556

commit v2 on v0

v2 whole, which is shorter than its diff:
```python
import math

import jax
import jax.numpy as jnp
from jax import lax
from jax.experimental import pallas as pl
from jax.experimental.pallas import tpu as pltpu
from jax.sharding import PartitionSpec as P

DH = 128
QBLK = 128
MAXB = 16
SEGB = 16
HALO = 3 * QBLK
CHUNK = 2 * QBLK
WIDE = HALO + CHUNK
MESH = pl.DeviceIdType.MESH
VMEM = pltpu.VMEM
BF16 = jnp.bfloat16
F32 = jnp.float32
DEAD = -3e38
FACTOR = 1.0 / math.sqrt(DH)
NT = (((1,), (1,)), ((), ()))


def aligned(start, size):
    return pl.ds(pl.multiple_of(start, QBLK), size)


def remote(src, dst, send, recv, **where):
    return pltpu.make_async_remote_copy(
        src_ref=src,
        dst_ref=dst,
        send_sem=send,
        recv_sem=recv,
        device_id=where,
        device_id_type=MESH,
    )


def greet(heads, blks):
    head, blk = lax.axis_index("head"), lax.axis_index("blk")
    barrier = pltpu.get_barrier_semaphore()
    for step in range(1, heads):
        pl.semaphore_signal(
            barrier, inc=1, device_id={"head": lax.rem(head + step, heads)}, device_id_type=MESH
        )
    for step in range(1, blks):
        pl.semaphore_signal(
            barrier, inc=1, device_id={"blk": lax.rem(blk + step, blks)}, device_id_type=MESH
        )
    pl.semaphore_wait(barrier, heads + blks - 2)


def mark_live(lists, live):
    blk = lax.axis_index("blk")
    mine = lists[pl.ds(pl.multiple_of(blk * SEGB, SEGB), SEGB), :]
    summary = lax.broadcasted_iota(jnp.int32, (SEGB, MAXB), 0) * SEGB
    owner = lax.broadcasted_iota(jnp.int32, (SEGB, QBLK), 0) * SEGB
    for block in range(SEGB):
        hit = jnp.where(mine[block : block + 1, :] == summary, 1.0, 0.0)
        seen = jnp.broadcast_to(jnp.max(hit, axis=1, keepdims=True), (SEGB, QBLK))
        far = owner < blk * SEGB + block - 3
        live[block // 2, :, pl.ds((block % 2) * QBLK, QBLK)] = jnp.where(far, seen, 0.0)


def attend(c, q, k, v, g, sk, sv, dq, dk, dv, dsk, dsv, kt, skt, live, scores, gprob):
    blk = lax.axis_index("blk")
    keys = sk.shape[0]
    exp2_factor = FACTOR * math.log2(math.e)
    slabs = [(s, CHUNK) for s in range(0, keys, CHUNK)]
    base = pl.multiple_of(c * CHUNK, CHUNK)
    here = pl.ds(base, CHUNK)
    window = pl.ds(base, WIDE)
    queries, grads = q[here, :], g[here, :]
    top = jnp.full((1, CHUNK), DEAD, F32)
    for start, size in slabs:
        raw = lax.dot_general(sk[pl.ds(start, size), :], queries, NT, preferred_element_type=F32)
        for sub in range(0, size, QBLK):
            alive = live[c, pl.ds((start + sub) // QBLK, 1), :] > 0.5
            masked = jnp.where(alive, raw[sub : sub + QBLK] * exp2_factor, DEAD)
            scores[pl.ds(start + sub, QBLK), :] = masked
            top = jnp.maximum(top, jnp.max(masked, axis=0, keepdims=True))
    key_row = lax.broadcasted_iota(jnp.int32, (WIDE, CHUNK), 0)
    query_row = lax.broadcasted_iota(jnp.int32, (WIDE, CHUNK), 1)
    alive = (
        (key_row <= query_row + HALO)
        & ((key_row >= QBLK) | (query_row < QBLK))
        & ((blk > 0) | (key_row + base >= HALO))
    )
    raw = lax.dot_general(k[window, :], queries, NT, preferred_element_type=F32)
    masked = jnp.where(alive, raw * exp2_factor, DEAD)
    scores[pl.ds(keys, WIDE), :] = masked
    top = jnp.maximum(top, jnp.max(masked, axis=0, keepdims=True))

    total = jnp.zeros((1, CHUNK), F32)
    dotted = jnp.zeros((1, CHUNK), F32)
    for start, size in slabs + [(keys, WIDE)]:
        there = v[window, :] if start == keys else sv[pl.ds(start, size), :]
        gp = lax.dot_general(there, grads, NT, preferred_element_type=F32)
        weight = jnp.exp2(scores[pl.ds(start, size), :] - top)
        scores[pl.ds(start, size), :] = weight
        gprob[pl.ds(start, size), :] = gp
        total += jnp.sum(weight, axis=0, keepdims=True)
        dotted += jnp.sum(weight * gp, axis=0, keepdims=True)
    inverse = 1.0 / total
    row_dot = dotted * inverse

    dq_t = jnp.zeros((DH, CHUNK), F32)
    for start, size in slabs + [(keys, WIDE)]:
        prob = scores[pl.ds(start, size), :] * inverse
        ds = (prob * (gprob[pl.ds(start, size), :] - row_dot)).astype(BF16)
        value_part = jnp.dot(prob.astype(BF16), grads, preferred_element_type=F32)
        key_part = jnp.dot(ds, queries, preferred_element_type=F32)
        if start == keys:
            dv[window, :] += value_part
            dk[window, :] += key_part
            turned = kt[:, window]
        else:
            dsv[pl.ds(start, size), :] += value_part
            dsk[pl.ds(start, size), :] += key_part
            turned = skt[:, pl.ds(start, size)]
        dq_t += jnp.dot(turned, ds, preferred_element_type=F32)
    dq[here, :] = (dq_t.T * FACTOR).astype(BF16)


def fused(
    heads, blks, lists, q, k, v, g, oq, ok, ov,
    lq, lk, lv, lg, sk, sv, dq, dk, dv, dsk, dsv, bk, bv, gk, gv, hk, hv, block_sum, kt, skt, live, scores, gprob,
    send_in, recv_in, send_first, recv_first, send_own, send_sum, recv_sum, send_halo, recv_halo,
    send_out, recv_out, keep_out, send_part, recv_part, send_edge, recv_edge,
):
    head, blk = lax.axis_index("head"), lax.axis_index("blk")
    part = q.shape[0]
    rows = heads * part
    keys = blks * QBLK
    rest = part - QBLK

    arrays = ((k, lk, HALO), (v, lv, HALO), (q, lq, 0), (g, lg, 0))

    def into(which, source, there):
        src, dst, skip = arrays[which]
        return remote(
            src.at[:, aligned(there * DH, DH)],
            dst.at[aligned(skip + source * part, part)],
            send_in.at[which, there],
            recv_in.at[which, source],
            head=there,
        )

    def first(which, there):
        src, dst, _ = arrays[which]
        return remote(
            src.at[pl.ds(0, QBLK), aligned(there * DH, DH)],
            dst.at[pl.ds(HALO, QBLK)],
            send_first.at[which, there],
            recv_first.at[which],
            head=there,
        )

    def second(which, there):
        src, dst, _ = arrays[which]
        return remote(
            src.at[pl.ds(QBLK, rest), aligned(there * DH, DH)],
            dst.at[pl.ds(HALO + QBLK, rest)],
            send_in.at[which, there],
            recv_in.at[which, 0],
            head=there,
        )

    def own(which):
        src, dst, skip = arrays[which]
        return pltpu.make_async_copy(
            src.at[:, aligned(head * DH, DH)], dst.at[aligned(skip + head * part, part)], send_own.at[which]
        )

    def other(step):
        return lax.rem(head + step, heads)

    greet(heads, blks)

    @pl.when(head == 0)
    def _():
        for step in range(1, heads):
            for which in range(2):
                first(which, step).start()
        for step in range(1, heads):
            for which in range(2):
                second(which, step).start()

    for which in range(4):
        own(which).start()

    @pl.when(head > 0)
    def _():
        for step in range(1, heads):
            for which in range(2):
                into(which, head, other(step)).start()

    for step in range(1, heads):
        for which in range(2, 4):
            into(which, head, other(step)).start()

    def arrive(which, source):
        @pl.when(head != source)
        def _():
            if which < 2 and isinstance(source, int) and source == 0:
                second(which, head).wait_recv()
            else:
                into(which, source, head).wait_recv()

    pairs = ((lk, sk), (lv, sv))

    def summary(which, owner, there):
        src, dst = pairs[which]
        return remote(
            src.at[pl.ds(HALO, QBLK)],
            dst.at[aligned(owner * QBLK, QBLK)],
            send_sum.at[which, there],
            recv_sum.at[which, owner],
            blk=there,
        )

    def halo(which, there):
        src, _ = pairs[which]
        return remote(
            src.at[pl.ds(rows, HALO)], src.at[pl.ds(0, HALO)], send_halo.at[which], recv_halo.at[which], blk=there
        )

    mark_live(lists, live)
    for ref in (dk, dv, dsk, dsv):
        ref[...] = jnp.zeros(ref.shape, ref.dtype)
    for which in range(4):
        own(which).wait()

    for which in range(2):
        @pl.when(head > 0)
        def _():
            first(which, head).wait_recv()

    for step in range(1, blks):
        @pl.when(blk + step < blks)
        def _():
            for which in range(2):
                summary(which, blk, blk + step).start()

    for which in range(2):
        src, dst = pairs[which]
        for owner in range(blks):
            @pl.when(owner > blk)
            def _():
                dst[pl.ds(owner * QBLK, QBLK), :] = jnp.zeros((QBLK, DH), BF16)

        dst[aligned(blk * QBLK, QBLK), :] = src[pl.ds(HALO, QBLK), :]

    for source in range(heads - 1, -1, -1):
        for which in range(2):
            arrive(which, source)
        if source == heads - 2:
            @pl.when(blk + 1 < blks)
            def _():
                for which in range(2):
                    halo(which, blk + 1).start()

    @pl.when(blk == 0)
    def _():
        for src, _ in pairs:
            src[pl.ds(0, HALO), :] = jnp.zeros((HALO, DH), BF16)

    @pl.when(blk > 0)
    def _():
        for which in range(2):
            halo(which, blk).wait_recv()

    for which in range(2):
        for owner in range(blks - 1):
            @pl.when(owner < blk)
            def _():
                summary(which, owner, blk).wait_recv()

    for start in range(0, HALO + rows, QBLK):
        kt[:, pl.ds(start, QBLK)] = lk[pl.ds(start, QBLK), :].T
    for start in range(0, keys, QBLK):
        skt[:, pl.ds(start, QBLK)] = sk[pl.ds(start, QBLK), :].T

    outs = ((dq, oq, 0), (bk, ok, HALO), (bv, ov, HALO))
    sets = ((dk, dsk, bk, gk, hk, FACTOR), (dv, dsv, bv, gv, hv, 1.0))

    def back(which, source, there):
        src, dst, skip = outs[which]
        return remote(
            src.at[aligned(skip + there * part, part)],
            dst.at[:, aligned(source * DH, DH)],
            send_out.at[which, there],
            recv_out.at[which, source],
            head=there,
        )

    def keep(which):
        src, dst, skip = outs[which]
        return pltpu.make_async_copy(
            src.at[aligned(skip + head * part, part)], dst.at[:, aligned(head * DH, DH)], keep_out.at[which]
        )

    def send(which, there):
        @pl.when(head != there)
        def _():
            back(which, head, there).start()

        @pl.when(head == there)
        def _():
            keep(which).start()

    def partial(which, owner, source):
        sums = sets[which][3]
        return remote(
            sums.at[0, aligned(owner * QBLK, QBLK)],
            sums.at[1, aligned(source * QBLK, QBLK)],
            send_part.at[which, owner],
            recv_part.at[which, source],
            blk=owner,
        )

    def edge(which, there):
        _, _, out, _, from_next, _ = sets[which]
        return remote(out.at[pl.ds(0, HALO)], from_next, send_edge.at[which], recv_edge.at[which], blk=there)

    def finish(which, there):
        acc, _, out, _, _, scale = sets[which]
        at = aligned(HALO + there * part, part)
        out[at, :] = (acc[at, :] * scale).astype(BF16)
        send(1 + which, there)

    def outer(c):
        return (c == 0) | (c >= heads - 2)

    def step_of(step, carry):
        c = lax.rem(head - step + heads, heads)

        @pl.when(step > 0)
        def _():
            for which in range(2, 4):
                into(which, c, head).wait_recv()

        attend(c, lq, lk, lv, lg, sk, sv, dq, dk, dv, dsk, dsv, kt, skt, live, scores, gprob)
        send(0, c)

        @pl.when((step >= 2) & jnp.logical_not(outer(c)))
        def _():
            for which in range(2):
                finish(which, c)

        return carry

    lax.fori_loop(0, heads, step_of, 0)

    for which in range(2):
        acc, acc_sum, out, sums, _, scale = sets[which]
        sums[0] = (acc_sum[...] * scale).astype(BF16)
        for owner in range(blks - 1):
            @pl.when(owner < blk)
            def _():
                partial(which, owner, blk).start()

        out[pl.ds(0, HALO), :] = (acc[pl.ds(0, HALO), :] * scale).astype(BF16)

        @pl.when(blk > 0)
        def _():
            edge(which, blk - 1).start()

    for step in range(2):
        c = lax.rem(head - step + heads, heads)

        @pl.when(jnp.logical_not(outer(c)))
        def _():
            for which in range(2):
                finish(which, c)

    for which in range(2):
        acc, _, out, _, from_next, scale = sets[which]
        spare = 2 * part - HALO
        at = pl.ds(HALO + rows - 2 * part, spare)
        out[at, :] = (acc[at, :] * scale).astype(BF16)
        at = pl.ds(rows, HALO)

        @pl.when(blk + 1 < blks)
        def _():
            edge(which, blk).wait_recv()
            out[at, :] = (acc[at, :] * scale + from_next[...].astype(F32)).astype(BF16)

        @pl.when(blk + 1 == blks)
        def _():
            out[at, :] = (acc[at, :] * scale).astype(BF16)

        for there in range(heads - 2, heads):
            send(1 + which, there)

    for which in range(2):
        acc, acc_sum, out, sums, _, scale = sets[which]
        block_sum[...] = (acc[pl.ds(HALO, QBLK), :] + acc_sum[aligned(blk * QBLK, QBLK), :]) * scale
        for source in range(1, blks):
            @pl.when(source > blk)
            def _():
                partial(which, blk, source).wait_recv()
                block_sum[...] += sums[1, pl.ds(source * QBLK, QBLK), :].astype(F32)

        out[pl.ds(HALO, QBLK), :] = block_sum[...].astype(BF16)
        at = pl.ds(HALO + QBLK, rest)
        out[at, :] = (acc[at, :] * scale).astype(BF16)
        send(1 + which, 0)

    @pl.when(head == 0)
    def _():
        for step in range(1, heads):
            for which in range(2):
                first(which, step).wait_send()
                second(which, step).wait_send()

    @pl.when(head > 0)
    def _():
        for step in range(1, heads):
            for which in range(2):
                into(which, head, other(step)).wait_send()

    for step in range(1, heads):
        for which in range(2, 4):
            into(which, head, other(step)).wait_send()

    for which in range(2):
        for step in range(1, blks):
            @pl.when(blk + step < blks)
            def _():
                summary(which, blk, blk + step).wait_send()

        for owner in range(blks - 1):
            @pl.when(owner < blk)
            def _():
                partial(which, owner, blk).wait_send()

        @pl.when(blk + 1 < blks)
        def _():
            halo(which, blk + 1).wait_send()

        @pl.when(blk > 0)
        def _():
            edge(which, blk - 1).wait_send()

    for which in range(3):
        keep(which).wait()
        for step in range(1, heads):
            back(which, head, other(step)).wait_send()
            back(which, other(step), head).wait_recv()


def body_of(heads, blks):
    def body(queries, key_in, values, grad_out, block_list):
        part, width = queries.shape
        rows, keys = heads * part, blks * QBLK
        dma = pltpu.SemaphoreType.DMA
        whole = pl.BlockSpec(memory_space=VMEM)
        far = pl.BlockSpec(memory_space=pltpu.HBM)
        return pl.pallas_call(
            lambda *refs: fused(heads, blks, *refs),
            out_shape=(jax.ShapeDtypeStruct((part, width), BF16),) * 3,
            in_specs=[whole] + [far] * 4,
            out_specs=[far] * 3,
            scratch_shapes=[
                VMEM((rows, DH), BF16),
                VMEM((HALO + rows, DH), BF16),
                VMEM((HALO + rows, DH), BF16),
                VMEM((rows, DH), BF16),
                VMEM((keys, DH), BF16),
                VMEM((keys, DH), BF16),
                VMEM((rows, DH), BF16),
                VMEM((HALO + rows, DH), F32),
                VMEM((HALO + rows, DH), F32),
                VMEM((keys, DH), F32),
                VMEM((keys, DH), F32),
                VMEM((HALO + rows, DH), BF16),
                VMEM((HALO + rows, DH), BF16),
                VMEM((2, keys, DH), BF16),
                VMEM((2, keys, DH), BF16),
                VMEM((HALO, DH), BF16),
                VMEM((HALO, DH), BF16),
                VMEM((QBLK, DH), F32),
                VMEM((DH, HALO + rows), BF16),
                VMEM((DH, keys), BF16),
                VMEM((rows // CHUNK, SEGB, CHUNK), F32),
                VMEM((keys + WIDE, CHUNK), F32),
                VMEM((keys + WIDE, CHUNK), F32),
                dma((4, heads)),
                dma((4, heads)),
                dma((2, heads)),
                dma((2,)),
                dma((4,)),
                dma((2, blks)),
                dma((2, blks)),
                dma((2,)),
                dma((2,)),
                dma((3, heads)),
                dma((3, heads)),
                dma((3,)),
                dma((2, blks)),
                dma((2, blks)),
                dma((2,)),
                dma((2,)),
            ],
            compiler_params=pltpu.CompilerParams(
                collective_id=0, has_side_effects=True, vmem_limit_bytes=62 * 1024 * 1024
            ),
            name="attention_backward",
        )(block_list, queries, key_in, values, grad_out)

    return body


def solution(mesh):
    placed = P(("blk", "head"), None)
    return jax.shard_map(
        body_of(mesh.shape["head"], mesh.shape["blk"]),
        mesh=mesh,
        in_specs=(placed,) * 4 + (P(),),
        out_specs=(placed,) * 3,
        check_vma=False,
    )
```

time: 660 us -> 115 us (0.17); the launches traced: 652 us -> 115 us
  waiting for transfers between devices: 359 us -> 0 us
  Pallas kernels: 0 us -> 109 us
  other arithmetic: 101 us -> 0 us
  local copies, waits for them, and re-layouts: 87.9 us -> 5.43 us
  matrix products: 54.9 us -> 0 us
  starting transfers between devices: 23.3 us -> 0 us
  between operations: 14.3 us -> 0.65 us
  blocking collectives: 12.7 us -> 0 us
    unnamed x3 -> x0, waiting for transfers between devices: 235 us -> none
    pallas_call x0 -> x1, Pallas kernels: none -> 109 us  [body(): pl.pallas_call(lambda *refs: fused(heads, blks, *refs), out_shape=(jax.Sh...]
    all_gather x1 -> x0, waiting for transfers between devices: 92.9 us -> none  [body(): kv_table = lax.all_gather(own_pair, 'blk', axis=1, tiled=True)]
    scatter-add x1 -> x0, other arithmetic: 73 us -> none  [body(): buffer = jnp.zeros((2, kv_table.shape[1], QBLK, row_width), jnp.float32)....]
    dot_general x6 -> x0, matrix products: 54.9 us -> none  [the longest x1 11.3 us: body(): jnp.einsum('sqhd,smkhd->shqmk', query_blocks, keys_sel, preferred_element...]
    unnamed x18 -> x8, local copies, waits for them, and re-layouts: 43.8 us -> 5.43 us
    all_to_all x6 -> x0, waiting for transfers between devices: 31.1 us -> none  [the longest x1 9.83 us: body(): lax.all_to_all(values, 'head', split_axis=1, concat_axis=0, tiled=True)]
    all_to_all x6 -> x0, starting transfers between devices: 23 us -> none  [the longest x1 5.03 us: body(): lax.all_to_all(key_in, 'head', split_axis=1, concat_axis=0, tiled=True)]
  transfers between devices with their start and end apart: 8 -> 0, of which waited for: 6 -> 0; matrix products, arithmetic and copies ran while one was open for 8% -> 0% of each run, Pallas kernels for 0% -> 0%
where the time goes in v2:
time: 115 us
  Pallas kernels  109 us (95%)
  local copies, waits for them, and re-layouts  5.43 us (5%)
    pallas_call x1, Pallas kernels, body(): pl.pallas_call(lambda *refs: fused(heads, blks, *refs), out_shape=(jax.Sh...  109 us
    unnamed x8, local copies, waits for them, and re-layouts  5.43 us

profile of v2, /device:TPU:97, one launch (start us, length us, event | category | flops | bytes accessed | tf_op | source)
XLA Modules:
  0.0 114.7 jit_solution(14578269969974997450)
XLA Ops:
  0.6 1.5 %copy.8.refs_0_ = s32[256,16]{1,0:T(8,128)} copy(s32[256,16]{0,1:T(8,128)} %param.9) | data formatting | bytes 32768 | tf_op args[4]
  2.1 108.7 %attention_backward.1 = (bf16[256,1024]{1,0:T(8,128)(2,1)}, bf16[256,1024]{1,0:T(8,128)(2,1)}, bf16[256,1024]{1,0:T(8,128)(2,1)}) custom-call(s32[256,16]{1,0:T(8,128)} %copy.8.refs_0_, bf16[256,1024]{1,0:T(8,128)(2,1)} %refs_1_.1, bf16[256,1024]{1,0:T(8,128)(2,1)} %refs_2_.1, bf16[256,1024]{1,0:T(8,128)(2,1)} %refs_3_.1, bf16[256,1024]{1,0:T(8,128)(2,1)} %refs_4_.1), custom_call_target="tpu_custom_call" | custom-call | tf_op jit(solution)/shard_map/attention_backward/pallas_call | solution.py:462
  110.8 0.0 copy-start.1
  110.8 1.9 %copy.12 = bf16[256,1024]{1,0:T(8,128)(2,1)} copy(bf16[256,1024]{1,0:T(8,128)(2,1)} %get-tuple-element.6) | data formatting | bytes 1048576
  112.7 0.0 copy-done.1
  112.7 0.0 copy-start
  112.7 0.8 copy.13
  113.5 0.4 copy-done
  113.9 0.8 copy.14
Async XLA Ops:
  110.8 1.9 %copy-start.1 = (bf16[256,1024]{1,0:T(8,128)(2,1)S(1)}, bf16[256,1024]{1,0:T(8,128)(2,1)}, u32[]{:S(2)}) copy-start(bf16[256,1024]{1,0:T(8,128)(2,1)} %get-tuple-element.7) | copy-start | bytes 1572868
  112.7 1.2 %copy-start = (bf16[256,1024]{1,0:T(8,128)(2,1)S(1)}, bf16[256,1024]{1,0:T(8,128)(2,1)}, u32[]{:S(2)}) copy-start(bf16[256,1024]{1,0:T(8,128)(2,1)} %get-tuple-element.8) | copy-start | bytes 1572868

commit v3 on v2

v3 whole, which is shorter than its diff:
```python
import math

import jax
import jax.numpy as jnp
from jax import lax
from jax.experimental import pallas as pl
from jax.experimental.pallas import tpu as pltpu
from jax.sharding import PartitionSpec as P

DH = 128
QBLK = 128
MAXB = 16
SEGB = 16
HALO = 3 * QBLK
CHUNK = 2 * QBLK
WIDE = HALO + CHUNK
MESH = pl.DeviceIdType.MESH
VMEM = pltpu.VMEM
BF16 = jnp.bfloat16
F32 = jnp.float32
DEAD = -3e38
FACTOR = 1.0 / math.sqrt(DH)
NT = (((1,), (1,)), ((), ()))


def aligned(start, size):
    return pl.ds(pl.multiple_of(start, QBLK), size)


def remote(src, dst, send, recv, **where):
    return pltpu.make_async_remote_copy(
        src_ref=src,
        dst_ref=dst,
        send_sem=send,
        recv_sem=recv,
        device_id=where,
        device_id_type=MESH,
    )


def greet(heads, blks):
    head, blk = lax.axis_index("head"), lax.axis_index("blk")
    barrier = pltpu.get_barrier_semaphore()
    for step in range(1, heads):
        pl.semaphore_signal(
            barrier, inc=1, device_id={"head": lax.rem(head + step, heads)}, device_id_type=MESH
        )
    for step in range(1, blks):
        pl.semaphore_signal(
            barrier, inc=1, device_id={"blk": lax.rem(blk + step, blks)}, device_id_type=MESH
        )
    pl.semaphore_wait(barrier, heads + blks - 2)


def mark_live(lists, live):
    blk = lax.axis_index("blk")
    blocks = lists.shape[1]
    owner = lax.broadcasted_iota(jnp.int32, (SEGB, blocks), 0)
    seen = jnp.zeros((SEGB, blocks), F32)
    for entry in range(MAXB):
        seen = jnp.where(lists[entry : entry + 1, :] == owner * SEGB, 1.0, seen)
    column = lax.broadcasted_iota(jnp.int32, (blocks, CHUNK), 0)
    query = lax.broadcasted_iota(jnp.int32, (blocks, CHUNK), 1) // QBLK
    slot = lax.broadcasted_iota(jnp.int32, (SEGB, CHUNK), 0) * SEGB
    reader = lax.broadcasted_iota(jnp.int32, (SEGB, CHUNK), 1) // QBLK
    for c in range(live.shape[0]):
        first = blk * SEGB + 2 * c
        spread = jnp.where(column == query + first, 1.0, 0.0).astype(BF16)
        chosen = jnp.dot(seen.astype(BF16), spread, preferred_element_type=F32)
        live[c] = jnp.where(slot < reader + (first - 3), chosen, 0.0)


def attend(c, q, k, v, g, sk, sv, dq, dk, dv, dsk, dsv, kt, skt, live, scores, gprob):
    blk = lax.axis_index("blk")
    keys = sk.shape[0]
    exp2_factor = FACTOR * math.log2(math.e)
    slabs = [(s, CHUNK) for s in range(0, keys, CHUNK)]
    base = pl.multiple_of(c * CHUNK, CHUNK)
    here = pl.ds(base, CHUNK)
    window = pl.ds(base, WIDE)
    queries, grads = q[here, :], g[here, :]
    top = jnp.full((1, CHUNK), DEAD, F32)
    for start, size in slabs:
        raw = lax.dot_general(sk[pl.ds(start, size), :], queries, NT, preferred_element_type=F32)
        for sub in range(0, size, QBLK):
            alive = live[c, pl.ds((start + sub) // QBLK, 1), :] > 0.5
            masked = jnp.where(alive, raw[sub : sub + QBLK] * exp2_factor, DEAD)
            scores[pl.ds(start + sub, QBLK), :] = masked
            top = jnp.maximum(top, jnp.max(masked, axis=0, keepdims=True))
    key_row = lax.broadcasted_iota(jnp.int32, (WIDE, CHUNK), 0)
    query_row = lax.broadcasted_iota(jnp.int32, (WIDE, CHUNK), 1)
    alive = (
        (key_row <= query_row + HALO)
        & ((key_row >= QBLK) | (query_row < QBLK))
        & ((blk > 0) | (key_row + base >= HALO))
    )
    raw = lax.dot_general(k[window, :], queries, NT, preferred_element_type=F32)
    masked = jnp.where(alive, raw * exp2_factor, DEAD)
    scores[pl.ds(keys, WIDE), :] = masked
    top = jnp.maximum(top, jnp.max(masked, axis=0, keepdims=True))

    total = jnp.zeros((1, CHUNK), F32)
    dotted = jnp.zeros((1, CHUNK), F32)
    for start, size in slabs + [(keys, WIDE)]:
        there = v[window, :] if start == keys else sv[pl.ds(start, size), :]
        gp = lax.dot_general(there, grads, NT, preferred_element_type=F32)
        weight = jnp.exp2(scores[pl.ds(start, size), :] - top)
        scores[pl.ds(start, size), :] = weight
        gprob[pl.ds(start, size), :] = gp
        total += jnp.sum(weight, axis=0, keepdims=True)
        dotted += jnp.sum(weight * gp, axis=0, keepdims=True)
    inverse = 1.0 / total
    row_dot = dotted * inverse

    dq_t = jnp.zeros((DH, CHUNK), F32)
    for start, size in slabs + [(keys, WIDE)]:
        prob = scores[pl.ds(start, size), :] * inverse
        ds = (prob * (gprob[pl.ds(start, size), :] - row_dot)).astype(BF16)
        value_part = jnp.dot(prob.astype(BF16), grads, preferred_element_type=F32)
        key_part = jnp.dot(ds, queries, preferred_element_type=F32)
        if start == keys:
            dv[window, :] += value_part
            dk[window, :] += key_part
            turned = kt[:, window]
        else:
            dsv[pl.ds(start, size), :] += value_part
            dsk[pl.ds(start, size), :] += key_part
            turned = skt[:, pl.ds(start, size)]
        dq_t += jnp.dot(turned, ds, preferred_element_type=F32)
    dq[here, :] = (dq_t.T * FACTOR).astype(BF16)


def fused(
    heads, blks, lists, q, k, v, g, oq, ok, ov,
    lq, lg, kv, skv, dq, dk, dv, dsk, dsv, bk, bv, sums, edges, block_sum, kt, skt, live, scores, gprob,
    send_in, recv_in, send_first, recv_first, send_own, send_sum, recv_sum, send_pass, recv_pass, send_halo,
    recv_halo, send_out, recv_out, keep_out, send_late, recv_late, keep_late, send_part, recv_part, send_edge,
    recv_edge,
):
    head, blk = lax.axis_index("head"), lax.axis_index("blk")
    part = q.shape[0]
    rows = heads * part
    keys = blks * QBLK
    rest = part - QBLK
    chips = blks // 2
    chip, core = blk // 2, lax.rem(blk, 2)
    sibling = blk + 1 - 2 * core
    lk, lv = kv.at[0], kv.at[1]
    sk, sv = skv.at[0], skv.at[1]

    arrays = ((k, lk, HALO), (v, lv, HALO), (q, lq, 0), (g, lg, 0))

    def into(which, source, there):
        src, dst, skip = arrays[which]
        return remote(
            src.at[:, aligned(there * DH, DH)],
            dst.at[aligned(skip + source * part, part)],
            send_in.at[which, there],
            recv_in.at[which, source],
            head=there,
        )

    def first(which, there):
        src, dst, _ = arrays[which]
        return remote(
            src.at[pl.ds(0, QBLK), aligned(there * DH, DH)],
            dst.at[pl.ds(HALO, QBLK)],
            send_first.at[which, there],
            recv_first.at[which],
            head=there,
        )

    def second(which, there):
        src, dst, _ = arrays[which]
        return remote(
            src.at[pl.ds(QBLK, rest), aligned(there * DH, DH)],
            dst.at[pl.ds(HALO + QBLK, rest)],
            send_in.at[which, there],
            recv_in.at[which, 0],
            head=there,
        )

    def own(which):
        src, dst, skip = arrays[which]
        return pltpu.make_async_copy(
            src.at[:, aligned(head * DH, DH)], dst.at[aligned(skip + head * part, part)], send_own.at[which]
        )

    def other(step):
        return lax.rem(head + step, heads)

    def slot(owner):
        return skv.at[:, aligned(owner * QBLK, QBLK)]

    def summary(owner, there):
        return remote(
            kv.at[:, pl.ds(HALO, QBLK)],
            slot(owner),
            send_sum.at[there],
            recv_sum.at[owner],
            blk=there * 2 + core,
        )

    def direct():
        return remote(kv.at[:, pl.ds(HALO, QBLK)], slot(chip * 2), send_pass.at[blks], recv_pass.at[blks], blk=sibling)

    def passed(owner):
        return remote(slot(owner), slot(owner), send_pass.at[owner], recv_pass.at[owner], blk=sibling)

    def halo(there):
        return remote(kv.at[:, pl.ds(rows, HALO)], kv.at[:, pl.ds(0, HALO)], send_halo, recv_halo, blk=there)

    def arrive(which, source):
        @pl.when(head != source)
        def _():
            if which < 2 and isinstance(source, int) and source == 0:
                second(which, head).wait_recv()
            else:
                into(which, source, head).wait_recv()

    greet(heads, blks)

    @pl.when(head == 0)
    def _():
        for step in range(1, heads):
            for which in range(2):
                first(which, step).start()

    for which in range(4):
        own(which).start()
    mark_live(lists, live)

    for which in range(2):
        own(which).wait()

        @pl.when(head > 0)
        def _():
            first(which, head).wait_recv()

    for there in range(1, chips):
        @pl.when(there > chip)
        def _():
            summary(blk, there).start()

    @pl.when(core == 0)
    def _():
        direct().start()

    @pl.when(head == 0)
    def _():
        for step in range(1, heads):
            for which in range(2):
                second(which, step).start()

    @pl.when(head > 0)
    def _():
        for step in range(1, heads):
            for which in range(2):
                into(which, head, other(step)).start()

    for ref in (dk, dv, dsk, dsv):
        ref[...] = jnp.zeros(ref.shape, ref.dtype)
    for owner in range(blks):
        @pl.when(owner > blk)
        def _():
            skv[:, pl.ds(owner * QBLK, QBLK), :] = jnp.zeros((2, QBLK, DH), BF16)

    skv[:, aligned(blk * QBLK, QBLK), :] = kv[:, pl.ds(HALO, QBLK), :]

    @pl.when(blk == 0)
    def _():
        kv[:, pl.ds(0, HALO), :] = jnp.zeros((2, HALO, DH), BF16)

    for there in range(chips - 1):
        @pl.when(there < chip)
        def _():
            summary(there * 2 + core, chip).wait_recv()
            passed(there * 2 + core).start()

    for source in range(heads - 1, -1, -1):
        for which in range(2):
            arrive(which, source)
        if source == heads - 2:
            @pl.when(blk + 1 < blks)
            def _():
                halo(blk + 1).start()

    @pl.when(head == 0)
    def _():
        for step in range(1, heads):
            for which in range(2):
                first(which, step).wait_send()
                second(which, step).wait_send()

    @pl.when(head > 0)
    def _():
        for step in range(1, heads):
            for which in range(2):
                into(which, head, other(step)).wait_send()

    for step in range(1, heads):
        for which in range(2, 4):
            into(which, head, other(step)).start()

    for start in range(HALO, HALO + rows, QBLK):
        kt[:, pl.ds(start, QBLK)] = lk[pl.ds(start, QBLK), :].T

    @pl.when(blk > 0)
    def _():
        halo(blk).wait_recv()

    for start in range(0, HALO, QBLK):
        kt[:, pl.ds(start, QBLK)] = lk[pl.ds(start, QBLK), :].T

    for there in range(chips - 1):
        @pl.when(there < chip)
        def _():
            passed(there * 2 + 1 - core).wait_recv()

    @pl.when(core == 1)
    def _():
        direct().wait_recv()

    for start in range(0, keys, QBLK):
        skt[:, pl.ds(start, QBLK)] = sk[pl.ds(start, QBLK), :].T
    for which in range(2, 4):
        own(which).wait()

    outs = ((dq, oq, 0), (bk, ok, HALO), (bv, ov, HALO))
    sets = ((dk, dsk, bk, FACTOR), (dv, dsv, bv, 1.0))

    def back(which, source, there):
        src, dst, skip = outs[which]
        return remote(
            src.at[aligned(skip + there * part, part)],
            dst.at[:, aligned(source * DH, DH)],
            send_out.at[which, there],
            recv_out.at[which, source],
            head=there,
        )

    def back_second(which, source):
        src, dst, skip = outs[which]
        return remote(
            src.at[pl.ds(skip + QBLK, rest)],
            dst.at[pl.ds(QBLK, rest), aligned(source * DH, DH)],
            send_out.at[which, 0],
            recv_out.at[which, source],
            head=0,
        )

    def back_first(which, source):
        src, dst, skip = outs[which]
        return remote(
            src.at[pl.ds(skip, QBLK)],
            dst.at[pl.ds(0, QBLK), aligned(source * DH, DH)],
            send_late.at[which],
            recv_late.at[which, source],
            head=0,
        )

    def keep(which):
        src, dst, skip = outs[which]
        return pltpu.make_async_copy(
            src.at[aligned(skip + head * part, part)], dst.at[:, aligned(head * DH, DH)], keep_out.at[which]
        )

    def keep_second(which):
        src, dst, skip = outs[which]
        return pltpu.make_async_copy(
            src.at[pl.ds(skip + QBLK, rest)], dst.at[pl.ds(QBLK, rest), pl.ds(0, DH)], keep_out.at[which]
        )

    def keep_first(which):
        src, dst, skip = outs[which]
        return pltpu.make_async_copy(
            src.at[pl.ds(skip, QBLK)], dst.at[pl.ds(0, QBLK), pl.ds(0, DH)], keep_late.at[which]
        )

    def send(which, there):
        @pl.when(head != there)
        def _():
            back(which, head, there).start()

        @pl.when(head == there)
        def _():
            keep(which).start()

    def partial(owner, source):
        return remote(
            sums.at[0, :, aligned(owner * QBLK, QBLK)],
            sums.at[1, :, aligned(source * QBLK, QBLK)],
            send_part.at[owner],
            recv_part.at[source],
            blk=owner,
        )

    def edge(there):
        return remote(edges.at[0], edges.at[1], send_edge, recv_edge, blk=there)

    def finish(there):
        at = aligned(HALO + there * part, part)
        for which in range(2):
            acc, _, out, scale = sets[which]
            out[at, :] = (acc[at, :] * scale).astype(BF16)
            send(1 + which, there)

    def finish_second():
        at = pl.ds(HALO + QBLK, rest)
        for which in range(2):
            acc, _, out, scale = sets[which]
            out[at, :] = (acc[at, :] * scale).astype(BF16)

            @pl.when(head > 0)
            def _():
                back_second(1 + which, head).start()

            @pl.when(head == 0)
            def _():
                keep_second(1 + which).start()

    def send_edges():
        @pl.when(blk > 0)
        def _():
            for which in range(2):
                acc, _, _, scale = sets[which]
                edges[0, which] = (acc[pl.ds(0, HALO), :] * scale).astype(BF16)
            edge(blk - 1).start()

    def finish_last():
        @pl.when(blk + 1 < blks)
        def _():
            edge(blk).wait_recv()
            for which in range(2):
                acc, _, _, scale = sets[which]
                acc[pl.ds(rows, HALO), :] += edges[1, which].astype(F32) * (1.0 / scale)

        for there in range(heads - 2, heads):
            finish(there)

    def step_of(step, carry):
        c = lax.rem(head - step + heads, heads)

        @pl.when(step > 0)
        def _():
            for which in range(2, 4):
                into(which, c, head).wait_recv()

        attend(c, lq, lk, lv, lg, sk, sv, dq, dk, dv, dsk, dsv, kt, skt, live, scores, gprob)
        send(0, c)

        @pl.when((step >= 2) & (c > 0) & (c < heads - 2))
        def _():
            finish(c)

        @pl.when((step >= 2) & (c == 0))
        def _():
            finish_second()

        @pl.when((step > 0) & (c == 0))
        def _():
            send_edges()

        @pl.when((step == head + 3) & (head > 0))
        def _():
            finish_last()

        return carry

    lax.fori_loop(0, heads, step_of, 0)

    for which in range(2):
        _, acc_sum, _, scale = sets[which]
        sums[0, which] = (acc_sum[...] * scale).astype(BF16)
    for owner in range(blks - 1):
        @pl.when(owner < blk)
        def _():
            partial(owner, blk).start()

    @pl.when(head == 0)
    def _():
        send_edges()

    for step in range(2):
        c = lax.rem(head - step + heads, heads)

        @pl.when((c > 0) & (c < heads - 2))
        def _():
            finish(c)

        @pl.when(c == 0)
        def _():
            finish_second()

    @pl.when((head == 0) | (head > heads - 4))
    def _():
        finish_last()

    for which in range(2):
        acc, acc_sum, _, scale = sets[which]
        block_sum[which] = (acc[pl.ds(HALO, QBLK), :] + acc_sum[aligned(blk * QBLK, QBLK), :]) * scale
    for source in range(1, blks):
        @pl.when(source > blk)
        def _():
            partial(blk, source).wait_recv()
            block_sum[...] += sums[1, :, pl.ds(source * QBLK, QBLK), :].astype(F32)

    for which in range(2):
        out = sets[which][2]
        out[pl.ds(HALO, QBLK), :] = block_sum[which].astype(BF16)

        @pl.when(head > 0)
        def _():
            back_first(1 + which, head).start()

        @pl.when(head == 0)
        def _():
            keep_first(1 + which).start()

    for step in range(1, heads):
        for which in range(2, 4):
            into(which, head, other(step)).wait_send()

    for there in range(1, chips):
        @pl.when(there > chip)
        def _():
            summary(blk, there).wait_send()

    @pl.when(core == 0)
    def _():
        direct().wait_send()

    for there in range(chips - 1):
        @pl.when(there < chip)
        def _():
            passed(there * 2 + core).wait_send()

    for owner in range(blks - 1):
        @pl.when(owner < blk)
        def _():
            partial(owner, blk).wait_send()

    @pl.when(blk + 1 < blks)
    def _():
        halo(blk + 1).wait_send()

    @pl.when(blk > 0)
    def _():
        edge(blk - 1).wait_send()

    keep(0).wait()
    for step in range(1, heads):
        back(0, head, other(step)).wait_send()
        back(0, other(step), head).wait_recv()

    @pl.when(head == 0)
    def _():
        for which in range(1, 3):
            keep_second(which).wait()
            keep_first(which).wait()
            for there in range(1, heads):
                back(which, 0, there).wait_send()
                back_second(which, there).wait_recv()
                back_first(which, there).wait_recv()

    @pl.when(head > 0)
    def _():
        for which in range(1, 3):
            keep(which).wait()
            back_second(which, head).wait_send()
            back_first(which, head).wait_send()
            for there in range(1, heads):
                @pl.when(there != head)
                def _():
                    back(which, head, there).wait_send()
            for step in range(1, heads):
                back(which, other(step), head).wait_recv()


def copy_kernel(x, y, z, ox, oy, oz, sem):
    copies = [pltpu.make_async_copy(a, b, sem.at[i]) for i, (a, b) in enumerate(((x, ox), (y, oy), (z, oz)))]
    for copy in copies:
        copy.start()
    for copy in copies:
        copy.wait()


def body_of(heads, blks):
    def body(queries, key_in, values, grad_out, block_list):
        part, width = queries.shape
        rows, keys = heads * part, blks * QBLK
        dma = pltpu.SemaphoreType.DMA
        whole = pl.BlockSpec(memory_space=VMEM)
        far = pl.BlockSpec(memory_space=pltpu.HBM)
        result = (jax.ShapeDtypeStruct((part, width), BF16),) * 3
        found = pl.pallas_call(
            lambda *refs: fused(heads, blks, *refs),
            out_shape=result,
            in_specs=[whole] + [far] * 4,
            out_specs=[far] * 3,
            scratch_shapes=[
                VMEM((rows, DH), BF16),
                VMEM((rows, DH), BF16),
                VMEM((2, HALO + rows, DH), BF16),
                VMEM((2, keys, DH), BF16),
                VMEM((rows, DH), BF16),
                VMEM((HALO + rows, DH), F32),
                VMEM((HALO + rows, DH), F32),
                VMEM((keys, DH), F32),
                VMEM((keys, DH), F32),
                VMEM((HALO + rows, DH), BF16),
                VMEM((HALO + rows, DH), BF16),
                VMEM((2, 2, keys, DH), BF16),
                VMEM((2, 2, HALO, DH), BF16),
                VMEM((2, QBLK, DH), F32),
                VMEM((DH, HALO + rows), BF16),
                VMEM((DH, keys), BF16),
                VMEM((rows // CHUNK, SEGB, CHUNK), F32),
                VMEM((keys + WIDE, CHUNK), F32),
                VMEM((keys + WIDE, CHUNK), F32),
                dma((4, heads)),
                dma((4, heads)),
                dma((2, heads)),
                dma((2,)),
                dma((4,)),
                dma((blks // 2,)),
                dma((blks,)),
                dma((blks + 1,)),
                dma((blks + 1,)),
                dma,
                dma,
                dma((3, heads)),
                dma((3, heads)),
                dma((3,)),
                dma((3,)),
                dma((3, heads)),
                dma((3,)),
                dma((blks,)),
                dma((blks,)),
                dma,
                dma,
            ],
            compiler_params=pltpu.CompilerParams(
                collective_id=0, has_side_effects=True, vmem_limit_bytes=62 * 1024 * 1024
            ),
            name="attention_backward",
        )(block_list.T, queries, key_in, values, grad_out)
        return pl.pallas_call(
            copy_kernel,
            out_shape=result,
            in_specs=[far] * 3,
            out_specs=[far] * 3,
            scratch_shapes=[dma((3,))],
            name="results",
        )(*found)

    return body


def solution(mesh):
    placed = P(("blk", "head"), None)
    return jax.shard_map(
        body_of(mesh.shape["head"], mesh.shape["blk"]),
        mesh=mesh,
        in_specs=(placed,) * 4 + (P(),),
        out_specs=(placed,) * 3,
        check_vma=False,
    )
```

time: 115 us -> 136 us (1.18)
  Pallas kernels: 109 us -> 135 us
  local copies, waits for them, and re-layouts: 5.43 us -> 0 us
    pallas_call x1 -> x2, Pallas kernels: 109 us -> 135 us  [the longest x1 86.1 us: body(): pl.pallas_call(lambda *refs: fused(heads, blks, *refs), out_shape=result,...]
    unnamed x8 -> x0, local copies, waits for them, and re-layouts: 5.43 us -> none
where the time goes in v3:
time: 136 us; the launch traced here: 135 us
  Pallas kernels  135 us (99%)
    pallas_call x1, Pallas kernels, body(): pl.pallas_call(lambda *refs: fused(heads, blks, *refs), out_shape=result,...  86.1 us
    pallas_call x1, Pallas kernels, body(): pl.pallas_call(copy_kernel, out_shape=result, in_specs=[far] * 3, out_spe...  48.8 us

profile of v3, /device:TPU:97, one launch (start us, length us, event | category | flops | bytes accessed | tf_op | source)
XLA Modules:
  0.0 135.5 jit_solution(225474542782404410)
XLA Ops:
  0.6 86.1 %attention_backward.1 = (bf16[256,1024]{1,0:T(8,128)(2,1)}, bf16[256,1024]{1,0:T(8,128)(2,1)}, bf16[256,1024]{1,0:T(8,128)(2,1)}) custom-call(s32[16,256]{1,0:T(8,128)} %bitcast.1, bf16[256,1024]{1,0:T(8,128)(2,1)} %refs_1_.1, bf16[256,1024]{1,0:T(8,128)(2,1)} %refs_2_.1, bf16[256,1024]{1,0:T(8,128)(2,1)} %refs_3_.1, bf16[256,1024]{1,0:T(8,128)(2,1)} %refs_4_.1), custom_call_target="tpu_custom_call" | custom-call | tf_op jit(solution)/shard_map/attention_backward/pallas_call | solution.py:596
  86.7 48.8 %results.1 = (bf16[256,1024]{1,0:T(8,128)(2,1)}, bf16[256,1024]{1,0:T(8,128)(2,1)}, bf16[256,1024]{1,0:T(8,128)(2,1)}) custom-call(bf16[256,1024]{1,0:T(8,128)(2,1)} %get-tuple-element.6.x, bf16[256,1024]{1,0:T(8,128)(2,1)} %get-tuple-element.7.y, bf16[256,1024]{1,0:T(8,128)(2,1)} %get-tuple-element.8.z), custom_call_target="tpu_custom_call" | custom-call | tf_op jit(solution)/shard_map/results/pallas_call | solution.py:648

commit v4 on v3

v4 whole, which is shorter than its diff:
```python
import functools
import math

import jax
import jax.numpy as jnp
from jax import lax
from jax.experimental import pallas as pl
from jax.experimental.pallas import tpu as pltpu
from jax.sharding import PartitionSpec as P

DH = 128
QBLK = 128
MAXB = 16
SEGB = 16
HALO = 3 * QBLK
CHUNK = 2 * QBLK
WIDE = HALO + CHUNK
EARLY = 2
MESH = pl.DeviceIdType.MESH
VMEM = pltpu.VMEM
BF16 = jnp.bfloat16
F32 = jnp.float32
DEAD = -3e38
FACTOR = 1.0 / math.sqrt(DH)
NT = (((1,), (1,)), ((), ()))
TN = (((0,), (0,)), ((), ()))


def aligned(start, size):
    return pl.ds(pl.multiple_of(start, QBLK), size)


def remote(src, dst, send, recv, **where):
    return pltpu.make_async_remote_copy(
        src_ref=src,
        dst_ref=dst,
        send_sem=send,
        recv_sem=recv,
        device_id=where,
        device_id_type=MESH,
    )


def greet(heads, blks):
    head, blk = lax.axis_index("head"), lax.axis_index("blk")
    core = lax.rem(blk, 2)
    barrier = pltpu.get_barrier_semaphore()

    def signal(**where):
        pl.semaphore_signal(barrier, inc=1, device_id=where, device_id_type=MESH)

    for step in range(1, heads):
        signal(head=lax.rem(head + step, heads))
    for step in range(2, blks, 2):
        signal(blk=lax.rem(blk + step, blks))
    signal(blk=blk + 1 - 2 * core)
    near = blk - 1 + 2 * core
    has_near = (near >= 0) & (near < blks)

    @pl.when(has_near)
    def _():
        signal(blk=near)

    pl.semaphore_wait(barrier, heads - 1 + blks // 2 + has_near.astype(jnp.int32))


def mark_live(lists, live):
    blk = lax.axis_index("blk")
    blocks = lists.shape[1]
    chips = SEGB // 2

    def owner_of(shape):
        slot = lax.broadcasted_iota(jnp.int32, shape, 0)
        return 2 * lax.rem(slot, chips) + slot // chips

    owner = owner_of((SEGB, blocks))
    seen = jnp.zeros((SEGB, blocks), F32)
    for entry in range(MAXB):
        seen = jnp.where(lists[entry : entry + 1, :] == owner * SEGB, 1.0, seen)
    column = lax.broadcasted_iota(jnp.int32, (blocks, CHUNK), 0)
    query = lax.broadcasted_iota(jnp.int32, (blocks, CHUNK), 1) // QBLK
    slot = owner_of((SEGB, CHUNK)) * SEGB
    reader = lax.broadcasted_iota(jnp.int32, (SEGB, CHUNK), 1) // QBLK
    for c in range(live.shape[0]):
        first = blk * SEGB + 2 * c
        spread = jnp.where(column == query + first, 1.0, 0.0).astype(BF16)
        chosen = jnp.dot(seen.astype(BF16), spread, preferred_element_type=F32)
        live[c] = jnp.where(slot < reader + (first - 3), chosen, 0.0)


def attend(c, pairs, q, k, v, g, sk, sv, dq, dk, dv, dsk, dsv, live, scores, gprob):
    blk = lax.axis_index("blk")
    keys = sk.shape[0]
    exp2_factor = FACTOR * math.log2(math.e)
    starts = [half + s * CHUNK for half in (0, keys // 2) for s in range(pairs)]
    base = pl.multiple_of(c * CHUNK, CHUNK)
    here = pl.ds(base, CHUNK)
    window = pl.ds(base, WIDE)
    queries, grads = q[here, :], g[here, :]
    slabs = [(pl.ds(s, CHUNK), pl.ds(s, CHUNK), sk, sv, dsk, dsv) for s in starts]
    slabs.append((pl.ds(keys, WIDE), window, k, v, dk, dv))

    tops, totals, dots = [], [], []
    for (at, rows, keys_of, values_of, _, _), start in zip(slabs, starts + [None]):
        raw = lax.dot_general(keys_of[rows, :], queries, NT, preferred_element_type=F32) * exp2_factor
        gp = lax.dot_general(values_of[rows, :], grads, NT, preferred_element_type=F32)
        if start is None:
            key_row = lax.broadcasted_iota(jnp.int32, (WIDE, CHUNK), 0)
            query_row = lax.broadcasted_iota(jnp.int32, (WIDE, CHUNK), 1)
            alive = (
                (key_row <= query_row + HALO)
                & ((key_row >= QBLK) | (query_row < QBLK))
                & ((blk > 0) | (key_row + base >= HALO))
            )
            masked = jnp.where(alive, raw, DEAD)
        else:
            masked = jnp.concatenate(
                [
                    jnp.where(live[c, pl.ds((start + sub) // QBLK, 1), :] > 0.5, raw[sub : sub + QBLK], DEAD)
                    for sub in range(0, CHUNK, QBLK)
                ],
                axis=0,
            )
        top = jnp.max(masked, axis=0, keepdims=True)
        weight = jnp.exp2(masked - top)
        scores[at, :] = weight
        gprob[at, :] = gp
        tops.append(top)
        totals.append(jnp.sum(weight, axis=0, keepdims=True))
        dots.append(jnp.sum(weight * gp, axis=0, keepdims=True))

    top = functools.reduce(jnp.maximum, tops)
    shares = [jnp.exp2(t - top) for t in tops]
    total = sum(t * share for t, share in zip(totals, shares))
    inverse = 1.0 / total
    row_dot = sum(t * share for t, share in zip(dots, shares)) * inverse

    query_grad = jnp.zeros((CHUNK, DH), F32)
    for (at, rows, keys_of, _, dk_of, dv_of), share in zip(slabs, shares):
        prob = scores[at, :] * (share * inverse)
        ds = (prob * (gprob[at, :] - row_dot)).astype(BF16)
        dv_of[rows, :] += jnp.dot(prob.astype(BF16), grads, preferred_element_type=F32)
        dk_of[rows, :] += jnp.dot(ds, queries, preferred_element_type=F32)
        query_grad += lax.dot_general(ds, keys_of[rows, :], TN, preferred_element_type=F32)
    dq[here, :] = (query_grad * FACTOR).astype(BF16)


def fused(
    heads, blks, lists, q, k, v, g, oq, ok, ov,
    lq, lg, kv, skv, dq, dk, dv, dsk, dsv, bk, bv, hand, sums, edges, block_sum, live, scores, gprob,
    send_in, recv_in, send_first, recv_first, send_own, send_sum, recv_sum, send_pass, recv_pass, send_halo,
    recv_halo, send_out, recv_out, keep_out, send_late, recv_late, keep_late, send_hand, recv_hand, send_part,
    recv_part, send_edge, recv_edge,
):
    head, blk = lax.axis_index("head"), lax.axis_index("blk")
    part = q.shape[0]
    rows = heads * part
    keys = blks * QBLK
    rest = part - QBLK
    chips = blks // 2
    chip, core = blk // 2, lax.rem(blk, 2)
    sibling = blk + 1 - 2 * core
    lk, lv = kv.at[0], kv.at[1]
    sk, sv = skv.at[0], skv.at[1]

    arrays = ((k, lk, HALO), (v, lv, HALO), (q, lq, 0), (g, lg, 0))

    def into(which, source, there):
        src, dst, skip = arrays[which]
        return remote(
            src.at[:, aligned(there * DH, DH)],
            dst.at[aligned(skip + source * part, part)],
            send_in.at[which, there],
            recv_in.at[which, source],
            head=there,
        )

    def first(which, there):
        src, dst, _ = arrays[which]
        return remote(
            src.at[pl.ds(0, QBLK), aligned(there * DH, DH)],
            dst.at[pl.ds(HALO, QBLK)],
            send_first.at[which, there],
            recv_first.at[which],
            head=there,
        )

    def second(which, there):
        src, dst, _ = arrays[which]
        return remote(
            src.at[pl.ds(QBLK, rest), aligned(there * DH, DH)],
            dst.at[pl.ds(HALO + QBLK, rest)],
            send_in.at[which, there],
            recv_in.at[which, 0],
            head=there,
        )

    def own(which):
        src, dst, skip = arrays[which]
        return pltpu.make_async_copy(
            src.at[:, aligned(head * DH, DH)], dst.at[aligned(skip + head * part, part)], send_own.at[which]
        )

    def other(step):
        return lax.rem(head + step, heads)

    def chunk_at(step):
        return lax.rem(head - step + heads, heads)

    place = chunk_at

    def done_at(c):
        late = jnp.maximum(place(c), place(jnp.minimum(c + 1, heads - 1)))
        return jnp.maximum(late, place(jnp.minimum(c + 2, heads - 1)))

    def slot(place_of, of_chip):
        return skv.at[:, aligned((place_of * chips + of_chip) * QBLK, QBLK)]

    def summary(of_chip, there):
        return remote(
            kv.at[:, pl.ds(HALO, QBLK)],
            slot(core, of_chip),
            send_sum.at[there],
            recv_sum.at[of_chip],
            blk=there * 2 + core,
        )

    def direct():
        return remote(
            kv.at[:, pl.ds(HALO, QBLK)], slot(0, chip), send_pass.at[chips], recv_pass.at[chips], blk=sibling
        )

    def passed(place_of, of_chip):
        return remote(
            slot(place_of, of_chip), slot(place_of, of_chip), send_pass.at[of_chip], recv_pass.at[of_chip], blk=sibling
        )

    def halo(there):
        return remote(kv.at[:, pl.ds(rows, HALO)], kv.at[:, pl.ds(0, HALO)], send_halo, recv_halo, blk=there)

    def arrive(which, source):
        @pl.when(head != source)
        def _():
            if which < 2 and isinstance(source, int) and source == 0:
                second(which, head).wait_recv()
            else:
                into(which, source, head).wait_recv()

    def drain_keys():
        @pl.when(head == 0)
        def _():
            for step in range(1, heads):
                for which in range(2):
                    first(which, step).wait_send()
                    second(which, step).wait_send()

        @pl.when(head > 0)
        def _():
            for step in range(1, heads):
                for which in range(2):
                    into(which, head, other(step)).wait_send()

    def drain_queries():
        for step in range(1, heads):
            for which in range(2, 4):
                into(which, head, other(step)).wait_send()

    def drain_summary():
        for there in range(1, chips):
            @pl.when(there > chip)
            def _():
                summary(chip, there).wait_send()

        @pl.when(core == 0)
        def _():
            direct().wait_send()

        for there in range(chips - 1):
            @pl.when(there < chip)
            def _():
                passed(core, there).wait_send()

        @pl.when(blk + 1 < blks)
        def _():
            halo(blk + 1).wait_send()

    greet(heads, blks)

    for which in range(4):
        own(which).start()

    @pl.when(head == 0)
    def _():
        for which in range(2):
            for step in range(1, heads):
                first(which, step).start()

    def send_keys(which):
        @pl.when(head == 0)
        def _():
            for step in range(1, heads):
                second(which, step).start()

        @pl.when(head > 0)
        def _():
            for step in range(1, heads):
                into(which, head, other(step)).start()

    send_keys(0)
    mark_live(lists, live)

    for which in range(2):
        own(which).wait()

        @pl.when(head > 0)
        def _():
            first(which, head).wait_recv()

    @pl.when(core == 0)
    def _():
        direct().start()

    for there in range(1, chips):
        @pl.when(there > chip)
        def _():
            summary(chip, there).start()

    send_keys(1)
    for step in range(1, 1 + EARLY):
        for which in range(2, 4):
            into(which, head, other(step)).start()

    for ref in (dk, dv, dsk, dsv):
        ref[...] = jnp.zeros(ref.shape, ref.dtype)
    nothing = jnp.zeros((2, QBLK, DH), BF16)
    for there in range(1, chips):
        @pl.when(there > chip)
        def _():
            for half in range(2):
                skv[:, pl.ds((half * chips + there) * QBLK, QBLK), :] = nothing

    @pl.when(core == 0)
    def _():
        skv[:, aligned((chips + chip) * QBLK, QBLK), :] = nothing

    skv[:, aligned((core * chips + chip) * QBLK, QBLK), :] = kv[:, pl.ds(HALO, QBLK), :]

    @pl.when(blk == 0)
    def _():
        kv[:, pl.ds(0, HALO), :] = jnp.zeros((2, HALO, DH), BF16)

    for there in range(chips - 1):
        @pl.when(there < chip)
        def _():
            summary(there, chip).wait_recv()
            passed(core, there).start()

    for source in range(heads - 1, -1, -1):
        for which in range(2):
            arrive(which, source)
        if source == heads - 2:
            @pl.when(blk + 1 < blks)
            def _():
                halo(blk + 1).start()

    drain_keys()
    for step in range(1 + EARLY, heads):
        for which in range(2, 4):
            into(which, head, other(step)).start()

    @pl.when(blk > 0)
    def _():
        halo(blk).wait_recv()

    for there in range(chips - 1):
        @pl.when(there < chip)
        def _():
            passed(1 - core, there).wait_recv()

    @pl.when(core == 1)
    def _():
        direct().wait_recv()

    for which in range(2, 4):
        own(which).wait()

    outs = ((dq, oq, 0), (bk, ok, HALO), (bv, ov, HALO))
    sets = ((dk, dsk, bk, FACTOR), (dv, dsv, bv, 1.0))

    def back(which, source, there):
        src, dst, skip = outs[which]
        return remote(
            src.at[aligned(skip + there * part, part)],
            dst.at[:, aligned(source * DH, DH)],
            send_out.at[which, there],
            recv_out.at[which, source],
            head=there,
        )

    def back_second(which, source):
        src, dst, skip = outs[which]
        return remote(
            src.at[pl.ds(skip + QBLK, rest)],
            dst.at[pl.ds(QBLK, rest), aligned(source * DH, DH)],
            send_out.at[which, 0],
            recv_out.at[which, source],
            head=0,
        )

    def back_first(which, source):
        src, dst, skip = outs[which]
        return remote(
            src.at[pl.ds(skip, QBLK)],
            dst.at[pl.ds(0, QBLK), aligned(source * DH, DH)],
            send_late.at[which],
            recv_late.at[which, source],
            head=0,
        )

    def keep(which):
        src, dst, skip = outs[which]
        return pltpu.make_async_copy(
            src.at[aligned(skip + head * part, part)], dst.at[:, aligned(head * DH, DH)], keep_out.at[which]
        )

    def keep_second(which):
        src, dst, skip = outs[which]
        return pltpu.make_async_copy(
            src.at[pl.ds(skip + QBLK, rest)], dst.at[pl.ds(QBLK, rest), pl.ds(0, DH)], keep_out.at[which]
        )

    def keep_first(which):
        src, dst, skip = outs[which]
        return pltpu.make_async_copy(
            src.at[pl.ds(skip, QBLK)], dst.at[pl.ds(0, QBLK), pl.ds(0, DH)], keep_late.at[which]
        )

    def send(which, there):
        @pl.when(head != there)
        def _():
            back(which, head, there).start()

        @pl.when(head == there)
        def _():
            keep(which).start()

    def handed():
        return remote(hand.at[0], hand.at[1], send_hand, recv_hand, blk=sibling)

    def partial(owner, source):
        return remote(
            sums.at[0, :, aligned(owner * QBLK, QBLK)],
            sums.at[1, :, aligned(source * QBLK, QBLK)],
            send_part.at[owner],
            recv_part.at[source],
            blk=owner * 2 + core,
        )

    def edge(there):
        return remote(edges.at[0], edges.at[1], send_edge, recv_edge, blk=there)

    def finish(there):
        at = aligned(HALO + there * part, part)
        for which in range(2):
            acc, _, out, scale = sets[which]
            out[at, :] = (acc[at, :] * scale).astype(BF16)
            send(1 + which, there)

    def finish_second():
        at = pl.ds(HALO + QBLK, rest)
        for which in range(2):
            acc, _, out, scale = sets[which]
            out[at, :] = (acc[at, :] * scale).astype(BF16)

            @pl.when(head > 0)
            def _():
                back_second(1 + which, head).start()

            @pl.when(head == 0)
            def _():
                keep_second(1 + which).start()

    def send_edges():
        @pl.when(blk > 0)
        def _():
            for which in range(2):
                acc, _, _, scale = sets[which]
                edges[0, which] = (acc[pl.ds(0, HALO), :] * scale).astype(BF16)
            edge(blk - 1).start()

    def finish_last():
        @pl.when(blk + 1 < blks)
        def _():
            edge(blk).wait_recv()
            for which in range(2):
                acc, _, _, scale = sets[which]
                acc[pl.ds(rows, HALO), :] += edges[1, which].astype(F32) * (1.0 / scale)

        for there in range(heads - 2, heads):
            finish(there)

    edges_at = jnp.maximum(place(0), place(1))
    last_at = jnp.maximum(edges_at + 2, jnp.maximum(place(heads - 2), place(heads - 1)))

    def step_of(step, carry):
        c = chunk_at(step)

        @pl.when(step > 0)
        def _():
            for which in range(2, 4):
                into(which, c, head).wait_recv()

        for pairs in range(1, chips // 2 + 1):
            @pl.when(chip // 2 + 1 == pairs)
            def _():
                attend(c, pairs, lq, lk, lv, lg, sk, sv, dq, dk, dv, dsk, dsv, live, scores, gprob)

        send(0, c)

        for back_by in range(3):
            ready = c - back_by

            @pl.when((ready > 0) & (ready < heads - 2) & (done_at(ready) == step))
            def _():
                finish(ready)

        @pl.when(done_at(0) == step)
        def _():
            finish_second()

        @pl.when(edges_at == step)
        def _():
            send_edges()

        @pl.when(last_at == step)
        def _():
            finish_last()

        return carry

    lax.fori_loop(0, heads, step_of, 0)

    half = chips * QBLK
    for which in range(2):
        _, acc_sum, _, scale = sets[which]
        hand[0, which] = (acc_sum[aligned((1 - core) * half, half), :] * scale).astype(BF16)
    handed().start()
    handed().wait_recv()
    for which in range(2):
        acc, acc_sum, _, scale = sets[which]
        for there in range(chips - 1):
            @pl.when(there < chip)
            def _():
                at = pl.ds(there * QBLK, QBLK)
                mine = acc_sum[aligned(core * half + there * QBLK, QBLK), :] * scale
                sums[0, which, at, :] = (mine + hand[1, which, at, :].astype(F32)).astype(BF16)

    for there in range(chips - 1):
        @pl.when(there < chip)
        def _():
            partial(there, chip).start()

    @pl.when(last_at >= heads)
    def _():
        finish_last()

    for which in range(2):
        acc, acc_sum, _, scale = sets[which]
        at = aligned(chip * QBLK, QBLK)
        mine = acc[pl.ds(HALO, QBLK), :] + acc_sum[aligned(core * half + chip * QBLK, QBLK), :]
        block_sum[which] = mine * scale + hand[1, which, at, :].astype(F32)
    for source in range(chips - 1, 0, -1):
        @pl.when(source > chip)
        def _():
            partial(chip, source).wait_recv()
            block_sum[...] += sums[1, :, pl.ds(source * QBLK, QBLK), :].astype(F32)

    for which in range(2):
        out = sets[which][2]
        out[pl.ds(HALO, QBLK), :] = block_sum[which].astype(BF16)

        @pl.when(head > 0)
        def _():
            back_first(1 + which, head).start()

        @pl.when(head == 0)
        def _():
            keep_first(1 + which).start()

    drain_queries()
    drain_summary()
    handed().wait_send()
    for there in range(chips - 1):
        @pl.when(there < chip)
        def _():
            partial(there, chip).wait_send()

    @pl.when(blk > 0)
    def _():
        edge(blk - 1).wait_send()

    keep(0).wait()
    for step in range(1, heads):
        back(0, head, other(step)).wait_send()
        back(0, other(step), head).wait_recv()

    @pl.when(head == 0)
    def _():
        for which in range(1, 3):
            keep_second(which).wait()
            keep_first(which).wait()
            for there in range(1, heads):
                back(which, 0, there).wait_send()
                back_second(which, there).wait_recv()
                back_first(which, there).wait_recv()

    @pl.when(head > 0)
    def _():
        for which in range(1, 3):
            keep(which).wait()
            back_second(which, head).wait_send()
            back_first(which, head).wait_send()
            for there in range(1, heads):
                @pl.when(there != head)
                def _():
                    back(which, head, there).wait_send()
            for step in range(1, heads):
                back(which, other(step), head).wait_recv()


def body_of(heads, blks):
    def body(queries, key_in, values, grad_out, block_list):
        part, width = queries.shape
        rows, keys = heads * part, blks * QBLK
        dma = pltpu.SemaphoreType.DMA
        whole = pl.BlockSpec(memory_space=VMEM)
        far = pl.BlockSpec(memory_space=pltpu.HBM)
        result = (jax.ShapeDtypeStruct((part, width), BF16),) * 3
        return pl.pallas_call(
            lambda *refs: fused(heads, blks, *refs),
            out_shape=result,
            in_specs=[whole] + [far] * 4,
            out_specs=[whole] * 3,
            scratch_shapes=[
                VMEM((rows, DH), BF16),
                VMEM((rows, DH), BF16),
                VMEM((2, HALO + rows, DH), BF16),
                VMEM((2, keys, DH), BF16),
                VMEM((rows, DH), BF16),
                VMEM((HALO + rows, DH), F32),
                VMEM((HALO + rows, DH), F32),
                VMEM((keys, DH), F32),
                VMEM((keys, DH), F32),
                VMEM((HALO + rows, DH), BF16),
                VMEM((HALO + rows, DH), BF16),
                VMEM((2, 2, keys // 2, DH), BF16),
                VMEM((2, 2, keys // 2, DH), BF16),
                VMEM((2, 2, HALO, DH), BF16),
                VMEM((2, QBLK, DH), F32),
                VMEM((rows // CHUNK, SEGB, CHUNK), F32),
                VMEM((keys + WIDE, CHUNK), F32),
                VMEM((keys + WIDE, CHUNK), F32),
                dma((4, heads)),
                dma((4, heads)),
                dma((2, heads)),
                dma((2,)),
                dma((4,)),
                dma((blks // 2,)),
                dma((blks // 2,)),
                dma((blks // 2 + 1,)),
                dma((blks // 2 + 1,)),
                dma,
                dma,
                dma((3, heads)),
                dma((3, heads)),
                dma((3,)),
                dma((3,)),
                dma((3, heads)),
                dma((3,)),
                dma,
                dma,
                dma((blks // 2,)),
                dma((blks // 2,)),
                dma,
                dma,
            ],
            compiler_params=pltpu.CompilerParams(
                collective_id=0, has_side_effects=True, vmem_limit_bytes=62 * 1024 * 1024
            ),
            name="attention_backward",
        )(block_list.T, queries, key_in, values, grad_out)

    return body


def solution(mesh):
    placed = P(("blk", "head"), None)
    return jax.shard_map(
        body_of(mesh.shape["head"], mesh.shape["blk"]),
        mesh=mesh,
        in_specs=(placed,) * 4 + (P(),),
        out_specs=(placed,) * 3,
        check_vma=False,
    )
```

time: 136 us -> 83 us (0.61)
  Pallas kernels: 135 us -> 77.7 us
  local copies, waits for them, and re-layouts: 0 us -> 3.95 us
    pallas_call x1 -> x0, Pallas kernels: 48.8 us -> none  [body(): pl.pallas_call(copy_kernel, out_shape=result, in_specs=[far] * 3, out_spe...]
    pallas_call x1, Pallas kernels: 86.1 us -> 77.7 us  [body(): pl.pallas_call(lambda *refs: fused(heads, blks, *refs), out_shape=result,...]
    unnamed x0 -> x7, local copies, waits for them, and re-layouts: none -> 3.95 us
where the time goes in v4:
time: 83 us; the launch traced here: 82.3 us
  Pallas kernels  77.7 us (94%)
  local copies, waits for them, and re-layouts  3.95 us (5%)
    pallas_call x1, Pallas kernels, body(): pl.pallas_call(lambda *refs: fused(heads, blks, *refs), out_shape=result,...  77.7 us
    unnamed x7, local copies, waits for them, and re-layouts  3.95 us

profile of v4, /device:TPU:97, one launch (start us, length us, event | category | flops | bytes accessed | tf_op | source)
XLA Modules:
  0.0 82.3 jit_solution(13566661964055892637)
XLA Ops:
  0.6 77.7 %attention_backward.1 = (bf16[256,1024]{1,0:T(8,128)(2,1)}, bf16[256,1024]{1,0:T(8,128)(2,1)}, bf16[256,1024]{1,0:T(8,128)(2,1)}) custom-call(s32[16,256]{1,0:T(8,128)} %bitcast.1, bf16[256,1024]{1,0:T(8,128)(2,1)} %refs_1_.1, bf16[256,1024]{1,0:T(8,128)(2,1)} %refs_2_.1, bf16[256,1024]{1,0:T(8,128)(2,1)} %refs_3_.1, bf16[256,1024]{1,0:T(8,128)(2,1)} %refs_4_.1), custom_call_target="tpu_custom_call" | custom-call | tf_op jit(solution)/shard_map/attention_backward/pallas_call | solution.py:639
  78.3 0.0 copy-start.1
  78.4 1.9 %copy.11 = bf16[256,1024]{1,0:T(8,128)(2,1)} copy(bf16[256,1024]{1,0:T(8,128)(2,1)} %get-tuple-element.6) | data formatting | bytes 1048576
  80.3 0.0 copy-done.1
  80.3 0.0 copy-start
  80.3 0.8 copy.12
  81.1 0.4 copy-done
  81.5 0.8 copy.13
Async XLA Ops:
  78.3 1.9 %copy-start.1 = (bf16[256,1024]{1,0:T(8,128)(2,1)S(1)}, bf16[256,1024]{1,0:T(8,128)(2,1)}, u32[]{:S(2)}) copy-start(bf16[256,1024]{1,0:T(8,128)(2,1)} %get-tuple-element.7) | copy-start | bytes 1572868
  80.3 1.2 %copy-start = (bf16[256,1024]{1,0:T(8,128)(2,1)S(1)}, bf16[256,1024]{1,0:T(8,128)(2,1)}, u32[]{:S(2)}) copy-start(bf16[256,1024]{1,0:T(8,128)(2,1)} %get-tuple-element.8) | copy-start | bytes 1572868

commit v5 on v4

--- a/solution.py
+++ b/solution.py
@@ -15,7 +15,6 @@
 HALO = 3 * QBLK
 CHUNK = 2 * QBLK
 WIDE = HALO + CHUNK
-EARLY = 2
 MESH = pl.DeviceIdType.MESH
 VMEM = pltpu.VMEM
 BF16 = jnp.bfloat16
@@ -88,7 +87,7 @@
         live[c] = jnp.where(slot < reader + (first - 3), chosen, 0.0)
 
 
-def attend(c, pairs, q, k, v, g, sk, sv, dq, dk, dv, dsk, dsv, live, scores, gprob):
+def attend(c, pairs, ready, summed, q, k, v, g, sk, sv, dq, dk, dv, dsk, dsv, live, scores, gprob):
     blk = lax.axis_index("blk")
     keys = sk.shape[0]
     exp2_factor = FACTOR * math.log2(math.e)
@@ -102,6 +101,8 @@
 
     tops, totals, dots = [], [], []
     for (at, rows, keys_of, values_of, _, _), start in zip(slabs, starts + [None]):
+        if start is None:
+            ready()
         raw = lax.dot_general(keys_of[rows, :], queries, NT, preferred_element_type=F32) * exp2_factor
         gp = lax.dot_general(values_of[rows, :], grads, NT, preferred_element_type=F32)
         if start is None:
@@ -137,6 +138,8 @@
 
     query_grad = jnp.zeros((CHUNK, DH), F32)
     for (at, rows, keys_of, _, dk_of, dv_of), share in zip(slabs, shares):
+        if keys_of is k:
+            summed()
         prob = scores[at, :] * (share * inverse)
         ds = (prob * (gprob[at, :] - row_dot)).astype(BF16)
         dv_of[rows, :] += jnp.dot(prob.astype(BF16), grads, preferred_element_type=F32)
@@ -326,9 +329,6 @@
             summary(chip, there).start()
 
     send_keys(1)
-    for step in range(1, 1 + EARLY):
-        for which in range(2, 4):
-            into(which, head, other(step)).start()
 
     for ref in (dk, dv, dsk, dsv):
         ref[...] = jnp.zeros(ref.shape, ref.dtype)
@@ -348,12 +348,6 @@
     @pl.when(blk == 0)
     def _():
         kv[:, pl.ds(0, HALO), :] = jnp.zeros((2, HALO, DH), BF16)
-
-    for there in range(chips - 1):
-        @pl.when(there < chip)
-        def _():
-            summary(there, chip).wait_recv()
-            passed(core, there).start()
 
     for source in range(heads - 1, -1, -1):
         for which in range(2):
@@ -364,13 +358,15 @@
                 halo(blk + 1).start()
 
     drain_keys()
-    for step in range(1 + EARLY, heads):
+    for step in range(1, heads):
         for which in range(2, 4):
             into(which, head, other(step)).start()
 
-    @pl.when(blk > 0)
-    def _():
-        halo(blk).wait_recv()
+    for there in range(chips - 1):
+        @pl.when(there < chip)
+        def _():
+            summary(there, chip).wait_recv()
+            passed(core, there).start()
 
     for there in range(chips - 1):
         @pl.when(there < chip)
@@ -502,6 +498,35 @@
     edges_at = jnp.maximum(place(0), place(1))
     last_at = jnp.maximum(edges_at + 2, jnp.maximum(place(heads - 2), place(heads - 1)))
 
+    halo_at = jnp.minimum(place(0), place(1))
+
+    def halo_for(step):
+        @pl.when((blk > 0) & (step == halo_at))
+        def _():
+            halo(blk).wait_recv()
+
+    half = chips * QBLK
+
+    def hand_over(step):
+        @pl.when(step == heads - 1)
+        def _():
+            for which in range(2):
+                _, acc_sum, _, scale = sets[which]
+                hand[0, which] = (acc_sum[aligned((1 - core) * half, half), :] * scale).astype(BF16)
+            handed().start()
+
+    def finish_at(step):
+        for back_by in range(3):
+            ready = chunk_at(step) - back_by
+
+            @pl.when((ready > 0) & (ready < heads - 2) & (done_at(ready) == step))
+            def _():
+                finish(ready)
+
+        @pl.when(done_at(0) == step)
+        def _():
+            finish_second()
+
     def step_of(step, carry):
         c = chunk_at(step)
 
@@ -513,26 +538,19 @@
         for pairs in range(1, chips // 2 + 1):
             @pl.when(chip // 2 + 1 == pairs)
             def _():
-                attend(c, pairs, lq, lk, lv, lg, sk, sv, dq, dk, dv, dsk, dsv, live, scores, gprob)
+                attend(c, pairs, lambda: halo_for(step), lambda: hand_over(step), lq, lk, lv, lg, sk, sv, dq, dk, dv, dsk, dsv, live, scores, gprob)
 
         send(0, c)
 
-        for back_by in range(3):
-            ready = c - back_by
-
-            @pl.when((ready > 0) & (ready < heads - 2) & (done_at(ready) == step))
-            def _():
-                finish(ready)
-
-        @pl.when(done_at(0) == step)
-        def _():
-            finish_second()
+        @pl.when(step < heads - 1)
+        def _():
+            finish_at(step)
 
         @pl.when(edges_at == step)
         def _():
             send_edges()
 
-        @pl.when(last_at == step)
+        @pl.when((last_at == step) & (step < heads - 1))
         def _():
             finish_last()
 
@@ -540,11 +558,6 @@
 
     lax.fori_loop(0, heads, step_of, 0)
 
-    half = chips * QBLK
-    for which in range(2):
-        _, acc_sum, _, scale = sets[which]
-        hand[0, which] = (acc_sum[aligned((1 - core) * half, half), :] * scale).astype(BF16)
-    handed().start()
     handed().wait_recv()
     for which in range(2):
         acc, acc_sum, _, scale = sets[which]
@@ -560,7 +573,9 @@
         def _():
             partial(there, chip).start()
 
-    @pl.when(last_at >= heads)
+    finish_at(heads - 1)
+
+    @pl.when(last_at >= heads - 1)
     def _():
         finish_last()
 
@@ -628,6 +643,28 @@
                 back(which, other(step), head).wait_recv()
 
 
+def copy_kernel(x, y, z, ox, oy, oz, held, read, written):
+    pieces = read.shape[1]
+    size = x.shape[0] // pieces
+
+    def moves(which, piece):
+        src, dst = ((x, ox), (y, oy), (z, oz))[which]
+        at = pl.ds(piece * size, size)
+        return (
+            pltpu.make_async_copy(src.at[at], held.at[which, at], read.at[which, piece]),
+            pltpu.make_async_copy(held.at[which, at], dst.at[at], written.at[which, piece]),
+        )
+
+    todo = [moves(which, piece) for piece in range(pieces) for which in range(3)]
+    for first, _ in todo:
+        first.start()
+    for first, second in todo:
+        first.wait()
+        second.start()
+    for _, second in todo:
+        second.wait()
+
+
 def body_of(heads, blks):
     def body(queries, key_in, values, grad_out, block_list):
         part, width = queries.shape
@@ -636,11 +673,11 @@
         whole = pl.BlockSpec(memory_space=VMEM)
         far = pl.BlockSpec(memory_space=pltpu.HBM)
         result = (jax.ShapeDtypeStruct((part, width), BF16),) * 3
-        return pl.pallas_call(
+        found = pl.pallas_call(
             lambda *refs: fused(heads, blks, *refs),
             out_shape=result,
             in_specs=[whole] + [far] * 4,
-            out_specs=[whole] * 3,
+            out_specs=[far] * 3,
             scratch_shapes=[
                 VMEM((rows, DH), BF16),
                 VMEM((rows, DH), BF16),
@@ -689,6 +726,15 @@
             ),
             name="attention_backward",
         )(block_list.T, queries, key_in, values, grad_out)
+        return pl.pallas_call(
+            copy_kernel,
+            out_shape=result,
+            in_specs=[far] * 3,
+            out_specs=[far] * 3,
+            scratch_shapes=[VMEM((3, part, width), BF16), dma((3, 2)), dma((3, 2))],
+            compiler_params=pltpu.CompilerParams(vmem_limit_bytes=62 * 1024 * 1024),
+            name="results",
+        )(*found)
 
     return body
 

time: 83 us -> 78.4 us (0.945)
  the two profiles are of different devices: /device:TPU:97 before, /device:TPU:1 now
where the time goes in v5:
time: 78.4 us; the launch traced here: 78.1 us
  Pallas kernels  77.5 us (99%)
    pallas_call x1, Pallas kernels, body(): pl.pallas_call(lambda *refs: fused(heads, blks, *refs), out_shape=result,...  75.3 us
    pallas_call x1, Pallas kernels, body(): pl.pallas_call(copy_kernel, out_shape=result, in_specs=[far] * 3, out_spe...  2.19 us

profile of v5, /device:TPU:1, one launch (start us, length us, event | category | flops | bytes accessed | tf_op | source)
XLA Modules:
  0.0 78.1 jit_solution(17618425446239387814)
XLA Ops:
  0.6 75.3 %attention_backward.1 = (bf16[256,1024]{1,0:T(8,128)(2,1)}, bf16[256,1024]{1,0:T(8,128)(2,1)}, bf16[256,1024]{1,0:T(8,128)(2,1)}) custom-call(s32[16,256]{1,0:T(8,128)} %bitcast.1, bf16[256,1024]{1,0:T(8,128)(2,1)} %refs_1_.1, bf16[256,1024]{1,0:T(8,128)(2,1)} %refs_2_.1, bf16[256,1024]{1,0:T(8,128)(2,1)} %refs_3_.1, bf16[256,1024]{1,0:T(8,128)(2,1)} %refs_4_.1), custom_call_target="tpu_custom_call" | custom-call | tf_op jit(solution)/shard_map/attention_backward/pallas_call | solution.py:676
  75.9 2.2 %results.1 = (bf16[256,1024]{1,0:T(8,128)(2,1)}, bf16[256,1024]{1,0:T(8,128)(2,1)}, bf16[256,1024]{1,0:T(8,128)(2,1)}) custom-call(bf16[256,1024]{1,0:T(8,128)(2,1)} %get-tuple-element.6.x, bf16[256,1024]{1,0:T(8,128)(2,1)} %get-tuple-element.7.y, bf16[256,1024]{1,0:T(8,128)(2,1)} %get-tuple-element.8.z), custom_call_target="tpu_custom_call" | custom-call | tf_op jit(solution)/shard_map/results/pallas_call | solution.py:729

commit v6 on v5

--- a/solution.py
+++ b/solution.py
@@ -87,7 +87,7 @@
         live[c] = jnp.where(slot < reader + (first - 3), chosen, 0.0)
 
 
-def attend(c, pairs, ready, summed, q, k, v, g, sk, sv, dq, dk, dv, dsk, dsv, live, scores, gprob):
+def attend(c, pairs, ready, q, k, v, g, sk, sv, dq, dk, dv, dsk, dsv, live, scores, gprob):
     blk = lax.axis_index("blk")
     keys = sk.shape[0]
     exp2_factor = FACTOR * math.log2(math.e)
@@ -138,8 +138,6 @@
 
     query_grad = jnp.zeros((CHUNK, DH), F32)
     for (at, rows, keys_of, _, dk_of, dv_of), share in zip(slabs, shares):
-        if keys_of is k:
-            summed()
         prob = scores[at, :] * (share * inverse)
         ds = (prob * (gprob[at, :] - row_dot)).astype(BF16)
         dv_of[rows, :] += jnp.dot(prob.astype(BF16), grads, preferred_element_type=F32)
@@ -358,8 +356,8 @@
                 halo(blk + 1).start()
 
     drain_keys()
-    for step in range(1, heads):
-        for which in range(2, 4):
+    for which in range(2, 4):
+        for step in range(1, heads):
             into(which, head, other(step)).start()
 
     for there in range(chips - 1):
@@ -507,14 +505,6 @@
 
     half = chips * QBLK
 
-    def hand_over(step):
-        @pl.when(step == heads - 1)
-        def _():
-            for which in range(2):
-                _, acc_sum, _, scale = sets[which]
-                hand[0, which] = (acc_sum[aligned((1 - core) * half, half), :] * scale).astype(BF16)
-            handed().start()
-
     def finish_at(step):
         for back_by in range(3):
             ready = chunk_at(step) - back_by
@@ -538,7 +528,7 @@
         for pairs in range(1, chips // 2 + 1):
             @pl.when(chip // 2 + 1 == pairs)
             def _():
-                attend(c, pairs, lambda: halo_for(step), lambda: hand_over(step), lq, lk, lv, lg, sk, sv, dq, dk, dv, dsk, dsv, live, scores, gprob)
+                attend(c, pairs, lambda: halo_for(step), lq, lk, lv, lg, sk, sv, dq, dk, dv, dsk, dsv, live, scores, gprob)
 
         send(0, c)
 
@@ -558,6 +548,10 @@
 
     lax.fori_loop(0, heads, step_of, 0)
 
+    for which in range(2):
+        _, acc_sum, _, scale = sets[which]
+        hand[0, which] = (acc_sum[aligned((1 - core) * half, half), :] * scale).astype(BF16)
+    handed().start()
     handed().wait_recv()
     for which in range(2):
         acc, acc_sum, _, scale = sets[which]

time: 78.4 us -> 77.4 us (0.987)
  the two profiles are of different devices: /device:TPU:1 before, /device:TPU:97 now
where the time goes in v6:
time: 77.4 us; the launch traced here: 76 us
  Pallas kernels  75.4 us (97%)
    pallas_call x1, Pallas kernels, body(): pl.pallas_call(lambda *refs: fused(heads, blks, *refs), out_shape=result,...  73.2 us
    pallas_call x1, Pallas kernels, body(): pl.pallas_call(copy_kernel, out_shape=result, in_specs=[far] * 3, out_spe...  2.19 us

profile of v6, /device:TPU:97, one launch (start us, length us, event | category | flops | bytes accessed | tf_op | source)
XLA Modules:
  0.0 76.0 jit_solution(6018369716786955725)
XLA Ops:
  0.6 73.2 %attention_backward.1 = (bf16[256,1024]{1,0:T(8,128)(2,1)}, bf16[256,1024]{1,0:T(8,128)(2,1)}, bf16[256,1024]{1,0:T(8,128)(2,1)}) custom-call(s32[16,256]{1,0:T(8,128)} %bitcast.1, bf16[256,1024]{1,0:T(8,128)(2,1)} %refs_1_.1, bf16[256,1024]{1,0:T(8,128)(2,1)} %refs_2_.1, bf16[256,1024]{1,0:T(8,128)(2,1)} %refs_3_.1, bf16[256,1024]{1,0:T(8,128)(2,1)} %refs_4_.1), custom_call_target="tpu_custom_call" | custom-call | tf_op jit(solution)/shard_map/attention_backward/pallas_call | solution.py:670
  73.8 2.2 %results.1 = (bf16[256,1024]{1,0:T(8,128)(2,1)}, bf16[256,1024]{1,0:T(8,128)(2,1)}, bf16[256,1024]{1,0:T(8,128)(2,1)}) custom-call(bf16[256,1024]{1,0:T(8,128)(2,1)} %get-tuple-element.6.x, bf16[256,1024]{1,0:T(8,128)(2,1)} %get-tuple-element.7.y, bf16[256,1024]{1,0:T(8,128)(2,1)} %get-tuple-element.8.z), custom_call_target="tpu_custom_call" | custom-call | tf_op jit(solution)/shard_map/results/pallas_call | solution.py:723

commit v7 on v6

--- a/solution.py
+++ b/solution.py
@@ -530,15 +530,15 @@
             def _():
                 attend(c, pairs, lambda: halo_for(step), lq, lk, lv, lg, sk, sv, dq, dk, dv, dsk, dsv, live, scores, gprob)
 
+        @pl.when(edges_at == step)
+        def _():
+            send_edges()
+
         send(0, c)
 
         @pl.when(step < heads - 1)
         def _():
             finish_at(step)
-
-        @pl.when(edges_at == step)
-        def _():
-            send_edges()
 
         @pl.when((last_at == step) & (step < heads - 1))
         def _():

time: 77.4 us -> 77.4 us (level)
  no operation moved by 1% of the time
where the time goes in v7:
time: 77.4 us; the launch traced here: 76 us
  Pallas kernels  75.4 us (97%)
    pallas_call x1, Pallas kernels, body(): pl.pallas_call(lambda *refs: fused(heads, blks, *refs), out_shape=result,...  73.2 us
    pallas_call x1, Pallas kernels, body(): pl.pallas_call(copy_kernel, out_shape=result, in_specs=[far] * 3, out_spe...  2.19 us

profile of v7, /device:TPU:97, one launch (start us, length us, event | category | flops | bytes accessed | tf_op | source)
XLA Modules:
  0.0 76.0 jit_solution(12655223111298196943)
XLA Ops:
  0.6 73.2 %attention_backward.1 = (bf16[256,1024]{1,0:T(8,128)(2,1)}, bf16[256,1024]{1,0:T(8,128)(2,1)}, bf16[256,1024]{1,0:T(8,128)(2,1)}) custom-call(s32[16,256]{1,0:T(8,128)} %bitcast.1, bf16[256,1024]{1,0:T(8,128)(2,1)} %refs_1_.1, bf16[256,1024]{1,0:T(8,128)(2,1)} %refs_2_.1, bf16[256,1024]{1,0:T(8,128)(2,1)} %refs_3_.1, bf16[256,1024]{1,0:T(8,128)(2,1)} %refs_4_.1), custom_call_target="tpu_custom_call" | custom-call | tf_op jit(solution)/shard_map/attention_backward/pallas_call | solution.py:670
  73.8 2.2 %results.1 = (bf16[256,1024]{1,0:T(8,128)(2,1)}, bf16[256,1024]{1,0:T(8,128)(2,1)}, bf16[256,1024]{1,0:T(8,128)(2,1)}) custom-call(bf16[256,1024]{1,0:T(8,128)(2,1)} %get-tuple-element.6.x, bf16[256,1024]{1,0:T(8,128)(2,1)} %get-tuple-element.7.y, bf16[256,1024]{1,0:T(8,128)(2,1)} %get-tuple-element.8.z), custom_call_target="tpu_custom_call" | custom-call | tf_op jit(solution)/shard_map/results/pallas_call | solution.py:723
